TPU v7x, 128 devices: a whole 4x4x4 slice. The times are simulated.
128 devices in a mesh: ctx: 8 (over x, z_lo), fsdp: 16 (over z_hi, y, core).
Axes of the slice: x: 4, y: 4, z: 4 (z_hi: 2, z_lo: 2; z = z_hi * 2 + z_lo), core: 2. Of those that a mesh axis runs over, the one named last changes fastest.
Arguments:
- hidden_in: bfloat16 [16, 1024, 2048], P('fsdp', 'ctx'), may hold values from -6 to 6
- cotangent: bfloat16 [16, 1024, 2048], P('fsdp', 'ctx'), may hold values from -6 to 6
- block_table: int32 [16, 16], P('fsdp'), may hold values from 0 to 15, as said below
- positions: int32 [16, 1024], P('fsdp', 'ctx'), may hold values from 0 to 2047, as said below
- query_weight: float32 [1, 2048, 2048], P(None, ('ctx', 'fsdp')), may hold values from -0.125 to 0.125
- key_weight: float32 [1, 2048, 256], P(None, ('ctx', 'fsdp')), may hold values from -0.125 to 0.125
- value_weight: float32 [1, 2048, 256], P(None, ('ctx', 'fsdp')), may hold values from -0.125 to 0.125
- output_weight: float32 [1, 2048, 2048], P(None, ('ctx', 'fsdp')), may hold values from -2 to 2
- gate_weight: float32 [1, 5632, 2048], P(None, ('ctx', 'fsdp')), may hold values from -0.125 to 0.125
- up_weight: float32 [1, 5632, 2048], P(None, ('ctx', 'fsdp')), may hold values from -0.125 to 0.125
- down_weight: float32 [1, 5632, 2048], P(None, ('ctx', 'fsdp')), may hold values from -0.078125 to 0.078125
- norm_gains: float32 [1, 2048, 2], P(None, ('ctx', 'fsdp')), may hold values from 0.5 to 1.5
- query_first: float32 [1, 2048, 2048], P(None, ('ctx', 'fsdp')), may hold values from -80 to 80
- key_first: float32 [1, 2048, 256], P(None, ('ctx', 'fsdp')), may hold values from -256 to 256
- value_first: float32 [1, 2048, 256], P(None, ('ctx', 'fsdp')), may hold values from -256 to 256
- output_first: float32 [1, 2048, 2048], P(None, ('ctx', 'fsdp')), may hold values from -6 to 6
- gate_first: float32 [1, 5632, 2048], P(None, ('ctx', 'fsdp')), may hold values from -32 to 32
- up_first: float32 [1, 5632, 2048], P(None, ('ctx', 'fsdp')), may hold values from -32 to 32
- down_first: float32 [1, 5632, 2048], P(None, ('ctx', 'fsdp')), may hold values from -48 to 48
- gains_first: float32 [1, 2048, 2], P(None, ('ctx', 'fsdp')), may hold values from -128 to 128
- query_second: float32 [1, 2048, 2048], P(None, ('ctx', 'fsdp')), may hold values from 425.984 to 6881.28
- key_second: float32 [1, 2048, 256], P(None, ('ctx', 'fsdp')), may hold values from 3932.16 to 62259.2
- value_second: float32 [1, 2048, 256], P(None, ('ctx', 'fsdp')), may hold values from 3932.16 to 62259.2
- output_second: float32 [1, 2048, 2048], P(None, ('ctx', 'fsdp')), may hold values from 1.6 to 27.2
- gate_second: float32 [1, 5632, 2048], P(None, ('ctx', 'fsdp')), may hold values from 52.4288 to 835.584
- up_second: float32 [1, 5632, 2048], P(None, ('ctx', 'fsdp')), may hold values from 52.4288 to 835.584
- down_second: float32 [1, 5632, 2048], P(None, ('ctx', 'fsdp')), may hold values from 154.0096 to 2457.6
- gains_second: float32 [1, 2048, 2], P(None, ('ctx', 'fsdp')), may hold values from 966.656 to 15564.8
Outputs:
- hidden_out: bfloat16 [16, 1024, 2048], P('fsdp', 'ctx')
- hidden_grad: float32 [16, 1024, 2048], P('fsdp', 'ctx')
- query_grad: float32 [1, 2048, 2048], P(None, ('ctx', 'fsdp'))
- query_update: float32 [1, 2048, 2048], P(None, ('ctx', 'fsdp'))
- query_momentum: float32 [1, 2048, 2048], P(None, ('ctx', 'fsdp'))
- query_variance: float32 [1, 2048, 2048], P(None, ('ctx', 'fsdp'))
- key_grad: float32 [1, 2048, 256], P(None, ('ctx', 'fsdp'))
- key_update: float32 [1, 2048, 256], P(None, ('ctx', 'fsdp'))
- key_momentum: float32 [1, 2048, 256], P(None, ('ctx', 'fsdp'))
- key_variance: float32 [1, 2048, 256], P(None, ('ctx', 'fsdp'))
- value_grad: float32 [1, 2048, 256], P(None, ('ctx', 'fsdp'))
- value_update: float32 [1, 2048, 256], P(None, ('ctx', 'fsdp'))
- value_momentum: float32 [1, 2048, 256], P(None, ('ctx', 'fsdp'))
- value_variance: float32 [1, 2048, 256], P(None, ('ctx', 'fsdp'))
- output_grad: float32 [1, 2048, 2048], P(None, ('ctx', 'fsdp'))
- output_update: float32 [1, 2048, 2048], P(None, ('ctx', 'fsdp'))
- output_momentum: float32 [1, 2048, 2048], P(None, ('ctx', 'fsdp'))
- output_variance: float32 [1, 2048, 2048], P(None, ('ctx', 'fsdp'))
- gate_grad: float32 [1, 5632, 2048], P(None, ('ctx', 'fsdp'))
- gate_update: float32 [1, 5632, 2048], P(None, ('ctx', 'fsdp'))
- gate_momentum: float32 [1, 5632, 2048], P(None, ('ctx', 'fsdp'))
- gate_variance: float32 [1, 5632, 2048], P(None, ('ctx', 'fsdp'))
- up_grad: float32 [1, 5632, 2048], P(None, ('ctx', 'fsdp'))
- up_update: float32 [1, 5632, 2048], P(None, ('ctx', 'fsdp'))
- up_momentum: float32 [1, 5632, 2048], P(None, ('ctx', 'fsdp'))
- up_variance: float32 [1, 5632, 2048], P(None, ('ctx', 'fsdp'))
- down_grad: float32 [1, 5632, 2048], P(None, ('ctx', 'fsdp'))
- down_update: float32 [1, 5632, 2048], P(None, ('ctx', 'fsdp'))
- down_momentum: float32 [1, 5632, 2048], P(None, ('ctx', 'fsdp'))
- down_variance: float32 [1, 5632, 2048], P(None, ('ctx', 'fsdp'))
- gains_grad: float32 [1, 2048, 2], P(None, ('ctx', 'fsdp'))
- gains_update: float32 [1, 2048, 2], P(None, ('ctx', 'fsdp'))
- gains_momentum: float32 [1, 2048, 2], P(None, ('ctx', 'fsdp'))
- gains_variance: float32 [1, 2048, 2], P(None, ('ctx', 'fsdp'))
Inputs may be any that keep to these rules, and one draw needn't show every extreme that they name: `block_table`: in each row, stored blocks 2c and 2c + 1 hold logical blocks b and 2 * 8 - 1 - b; every row is a permutation. `positions`: strictly rising in logical order; the first logical token of each sequence has 0, the last 2047.
All inputs are finite; a program needn't handle non-finite values.
Results may differ from a plain program's by a relative error of at most 0.024.
Values may be sent and summed in bfloat16 or wider, within the bound.
No kernel may reach another device: no remote copies, remote signals or barrier semaphores. Data moves between devices by JAX's collectives and lax.ppermute only.
A program may use at most 768 MiB of HBM per device.

v0:
```python
import math

import jax
import jax.numpy as jnp
from jax import lax
from jax.sharding import PartitionSpec as P

D = 2048
HEADS = 32
KV_HEADS = 4
HEAD = 64
FF = 5632
LAYERS = 1
STEP = 10


EPS = 1e-05
NEG = -1e30
BETA_ONE = 0.9
BETA_TWO = 0.95
ADAM_EPS = 1e-08
RATES = (0.1, 0.1, 0.1, 1.5, 0.1, 0.1, 0.066, 0.5)
DECAYS = (0.1, 0.1, 0.1, 0.1, 0.1, 0.1, 0.1, 0.0)
BY_COLUMN = (((1,), (1,)), ((), ()))
BY_ROW = (((0,), (0,)), ((), ()))


def rope_tables(places):
    half = HEAD // 2
    freqs = jnp.exp(jnp.arange(half, dtype=jnp.float32) * (-2.0 * math.log(10000.0) / HEAD))
    angles = places.astype(jnp.float32)[:, None] * freqs[None, :]
    return (jnp.cos(angles)[:, None, :], jnp.sin(angles)[:, None, :])


def rotate(vector, cosine, sine):
    half = vector.shape[-1] // 2
    first_half = vector[..., :half]
    second_half = vector[..., half:]
    return jnp.concatenate(
        [first_half * cosine - second_half * sine, second_half * cosine + first_half * sine], -1
    )


def rms_scale(values):
    return lax.rsqrt(jnp.mean(values * values, -1, keepdims=True) + EPS)


def norm_back(values, scale, gain, incoming):
    normed = values * scale
    weighted = incoming * gain
    through = scale * (weighted - normed * jnp.mean(weighted * normed, -1, keepdims=True))
    return (through, jnp.sum(incoming * normed, 0))


def adam_step(weight, first, second, grad, rate, decay):
    momentum = BETA_ONE * first + (1.0 - BETA_ONE) * grad
    variance = BETA_TWO * second + (1.0 - BETA_TWO) * grad * grad
    corrected = momentum / (1.0 - BETA_ONE**STEP)
    root = jnp.sqrt(variance / (1.0 - BETA_TWO**STEP))
    update = weight - rate * (corrected / (root + ADAM_EPS) + decay * weight)
    return (update, momentum, variance)


def attention_weights(pieces):
    return (
        lax.all_gather(pieces[0], ("ctx", "fsdp"), axis=0, tiled=True),
        lax.all_gather(pieces[1], ("ctx", "fsdp"), axis=0, tiled=True),
        lax.all_gather(pieces[2], ("ctx", "fsdp"), axis=0, tiled=True),
        lax.all_gather(pieces[3], ("ctx", "fsdp"), axis=0, tiled=True),
        lax.all_gather(pieces[4], ("ctx", "fsdp"), axis=0, tiled=True),
    )


def mlp_fold(pieces, folder, initial):
    return folder(
        initial,
        (
            lax.all_gather(pieces[0], ("ctx", "fsdp"), axis=0, tiled=True),
            lax.all_gather(pieces[1], ("ctx", "fsdp"), axis=0, tiled=True),
            lax.all_gather(pieces[2], ("ctx", "fsdp"), axis=0, tiled=True),
        ),
        jnp.int32(0),
    )


def body(
    hidden_in,
    cotangent,
    block_table,
    positions,
    query_weight,
    key_weight,
    value_weight,
    output_weight,
    gate_weight,
    up_weight,
    down_weight,
    norm_gains,
    query_first,
    key_first,
    value_first,
    output_first,
    gate_first,
    up_first,
    down_first,
    gains_first,
    query_second,
    key_second,
    value_second,
    output_second,
    gate_second,
    up_second,
    down_second,
    gains_second,
):
    weights = (
        query_weight,
        key_weight,
        value_weight,
        output_weight,
        gate_weight,
        up_weight,
        down_weight,
        norm_gains,
    )
    firsts = (
        query_first,
        key_first,
        value_first,
        output_first,
        gate_first,
        up_first,
        down_first,
        gains_first,
    )
    seconds = (
        query_second,
        key_second,
        value_second,
        output_second,
        gate_second,
        up_second,
        down_second,
        gains_second,
    )
    groups = HEADS // KV_HEADS
    kv_width = KV_HEADS * HEAD
    scale = HEAD ** (-0.5)
    tokens = hidden_in.shape[1]
    block_rows = tokens // 2
    rank = lax.axis_index("ctx")
    logical = (
        block_table[0][:, None] * block_rows + jnp.arange(block_rows, dtype=jnp.int32)[None, :]
    ).reshape(-1)
    own_order = lax.dynamic_slice_in_dim(logical, rank * tokens, tokens)
    allowed = logical[None, :] <= own_order[:, None]
    cosine, sine = rope_tables(positions[0])
    bf16 = jnp.bfloat16
    f32 = jnp.float32
    layer_index = 0
    attn_low = tuple(
        (
            w[layer_index].astype(bf16)
            for w in (query_weight, key_weight, value_weight, output_weight, norm_gains)
        )
    )
    mlp_low = tuple((w[layer_index].astype(bf16) for w in (gate_weight, up_weight, down_weight)))
    layer_pieces = [(attn_low, mlp_low)]
    state = hidden_in[0].astype(f32)
    layer_index = 0
    attn_low, mlp_low = layer_pieces[layer_index]
    query_full, key_full, value_full, output_full, gains_full = attention_weights(attn_low)
    gain_attn = gains_full[:, 0].astype(f32)
    gain_mlp = gains_full[:, 1].astype(f32)
    scale_one = rms_scale(state)
    normed_one = (state * scale_one * gain_attn).astype(bf16)
    queries = jnp.dot(normed_one, query_full, preferred_element_type=f32).reshape(
        tokens, HEADS, HEAD
    )
    keys = jnp.dot(normed_one, key_full, preferred_element_type=f32).reshape(tokens, KV_HEADS, HEAD)
    value_low = jnp.dot(normed_one, value_full, preferred_element_type=f32).astype(bf16)
    query_rot = rotate(queries, cosine, sine).astype(bf16).reshape(tokens, KV_HEADS, groups, HEAD)
    key_rot = rotate(keys, cosine, sine).astype(bf16).reshape(tokens, kv_width)
    key_all = lax.all_gather(key_rot, "ctx", axis=0, tiled=True)
    value_all = lax.all_gather(value_low, "ctx", axis=0, tiled=True)
    key_heads = key_all.reshape(-1, KV_HEADS, HEAD)
    value_heads = value_all.reshape(-1, KV_HEADS, HEAD)
    scores = jnp.einsum("tkgd,nkd->kgtn", query_rot, key_heads, preferred_element_type=f32) * scale
    scores = jnp.where(allowed, scores, NEG)
    peak = jnp.max(scores, -1, keepdims=True)
    expo = jnp.exp(scores - peak)
    total = jnp.sum(expo, -1, keepdims=True)
    probs = (expo / total).astype(bf16)
    logsum = peak + jnp.log(total)
    mixed = jnp.einsum("kgtn,nkd->tkgd", probs, value_heads, preferred_element_type=f32).reshape(
        tokens, D
    )
    mixed_low = mixed.astype(bf16)
    residual_one = state + jnp.dot(mixed_low, output_full, preferred_element_type=f32)
    scale_two = rms_scale(residual_one)
    normed_two = (residual_one * scale_two * gain_mlp).astype(bf16)
    rows_in = normed_two

    def forward_fold(carried, pieces, offset, rows_in=rows_in):
        gate = lax.dot_general(rows_in, pieces[0], BY_COLUMN, preferred_element_type=f32)
        up_proj = lax.dot_general(rows_in, pieces[1], BY_COLUMN, preferred_element_type=f32)
        hidden = (gate * jax.nn.sigmoid(gate) * up_proj).astype(bf16)
        return jnp.dot(hidden, pieces[2], preferred_element_type=f32)

    branch_zero = jnp.zeros((rows_in.shape[0], D), f32)
    branch = mlp_fold(mlp_low, forward_fold, branch_zero)
    saved = [
        (
            state,
            scale_one,
            normed_one,
            query_rot,
            key_rot,
            value_low,
            key_all,
            value_all,
            logsum,
            mixed,
            mixed_low,
            residual_one,
            scale_two,
            rows_in,
            gain_attn,
            gain_mlp,
        )
    ]
    state = residual_one + branch
    hidden_out = state.astype(bf16)
    grad = cotangent[0].astype(f32)
    gain_terms = [None] * LAYERS
    grad_parts = [None] * LAYERS
    for layer_index in reversed(range(LAYERS)):
        (
            state_in,
            scale_one,
            normed_one,
            query_rot,
            key_rot,
            value_low,
            kept_keys,
            kept_values,
            logsum,
            mixed,
            mixed_low,
            residual_one,
            scale_two,
            rows_in,
            gain_attn,
            gain_mlp,
        ) = saved[layer_index]
        attn_low, mlp_low = layer_pieces[layer_index]
        grad_low = grad.astype(bf16)
        grad_rows = grad_low
        unit_count = FF

        def backward_fold(carried, pieces, offset, rows_in=rows_in, grad_rows=grad_rows):
            gate = lax.dot_general(rows_in, pieces[0], BY_COLUMN, preferred_element_type=f32)
            up_proj = lax.dot_general(rows_in, pieces[1], BY_COLUMN, preferred_element_type=f32)
            sigmoid = jax.nn.sigmoid(gate)
            silu_gate = gate * sigmoid
            hidden = (silu_gate * up_proj).astype(bf16)
            dhidden = lax.dot_general(grad_rows, pieces[2], BY_COLUMN, preferred_element_type=f32)
            dgate = (dhidden * up_proj * sigmoid * (1.0 + gate * (1.0 - sigmoid))).astype(bf16)
            dup = (dhidden * silu_gate).astype(bf16)
            summed = jnp.dot(dgate, pieces[0], preferred_element_type=f32) + jnp.dot(
                dup, pieces[1], preferred_element_type=f32
            )
            return (summed, dgate, dup, hidden)

        hidden_zero = jnp.zeros((rows_in.shape[0], unit_count), bf16)
        initial = (jnp.zeros((rows_in.shape[0], D), f32), hidden_zero, hidden_zero, hidden_zero)
        dnormed_two, gate_all, up_all, hidden_all = mlp_fold(mlp_low, backward_fold, initial)
        mlp_grad = lax.psum_scatter(
            jnp.concatenate(
                [
                    lax.dot_general(gate_all, rows_in, BY_ROW, preferred_element_type=f32),
                    lax.dot_general(up_all, rows_in, BY_ROW, preferred_element_type=f32),
                    lax.dot_general(hidden_all, grad_rows, BY_ROW, preferred_element_type=f32),
                ],
                1,
            ),
            ("ctx", "fsdp"),
            scatter_dimension=0,
            tiled=True,
        )
        through_two, gain_two = norm_back(residual_one, scale_two, gain_mlp, dnormed_two)
        grad_one = grad + through_two
        attn_grad_low = grad_one.astype(bf16)
        query_full, key_full, value_full, output_full, gains_again = attention_weights(attn_low)
        dmixed = (
            lax.dot_general(attn_grad_low, output_full, BY_COLUMN, preferred_element_type=f32)
            .astype(bf16)
            .reshape(tokens, KV_HEADS, groups, HEAD)
        )
        key_all, value_all = (
            lax.all_gather(key_rot, "ctx", axis=0, tiled=True),
            lax.all_gather(value_low, "ctx", axis=0, tiled=True),
        )
        key_heads = key_all.reshape(-1, KV_HEADS, HEAD)
        value_heads = value_all.reshape(-1, KV_HEADS, HEAD)
        scores = (
            jnp.einsum("tkgd,nkd->kgtn", query_rot, key_heads, preferred_element_type=f32) * scale
        )
        scores = jnp.where(allowed, scores, NEG)
        probs_full = jnp.exp(scores - logsum)
        probs_low = probs_full.astype(bf16)
        dprobs = jnp.einsum("tkgd,nkd->kgtn", dmixed, value_heads, preferred_element_type=f32)
        delta = jnp.transpose(
            jnp.sum(dmixed.astype(f32) * mixed.reshape(tokens, KV_HEADS, groups, HEAD), -1),
            (1, 2, 0),
        )
        dscores = (probs_full * (dprobs - delta[..., None]) * scale).astype(bf16)
        dquery = jnp.einsum(
            "kgtn,nkd->tkgd", dscores, key_heads, preferred_element_type=f32
        ).reshape(tokens, HEADS, HEAD)
        dkey_part = jnp.einsum(
            "kgtn,tkgd->nkd", dscores, query_rot, preferred_element_type=f32
        ).reshape(-1, kv_width)
        dvalue_part = jnp.einsum(
            "kgtn,tkgd->nkd", probs_low, dmixed, preferred_element_type=f32
        ).reshape(-1, kv_width)
        dkey, dvalue = (
            lax.psum_scatter(
                dkey_part.astype(jnp.bfloat16), "ctx", scatter_dimension=0, tiled=True
            ).astype(jnp.float32),
            lax.psum_scatter(
                dvalue_part.astype(jnp.bfloat16), "ctx", scatter_dimension=0, tiled=True
            ).astype(jnp.float32),
        )
        dquery_low = rotate(dquery, cosine, -sine).astype(bf16).reshape(tokens, D)
        dkey_low = (
            rotate(dkey.reshape(tokens, KV_HEADS, HEAD), cosine, -sine)
            .astype(bf16)
            .reshape(tokens, kv_width)
        )
        dvalue_low = dvalue.astype(bf16)
        dnormed_one = (
            lax.dot_general(dquery_low, query_full, BY_COLUMN, preferred_element_type=f32)
            + lax.dot_general(dkey_low, key_full, BY_COLUMN, preferred_element_type=f32)
            + lax.dot_general(dvalue_low, value_full, BY_COLUMN, preferred_element_type=f32)
        )
        projected = jnp.concatenate([dquery_low, dkey_low, dvalue_low], 1)

        def attn_terms(
            offset,
            amount,
            normed_one=normed_one,
            mixed_low=mixed_low,
            projected=projected,
            attn_grad_low=attn_grad_low,
        ):
            return jnp.concatenate(
                [
                    lax.dot_general(normed_one, projected, BY_ROW, preferred_element_type=f32),
                    lax.dot_general(mixed_low, attn_grad_low, BY_ROW, preferred_element_type=f32),
                ],
                1,
            )

        attn_grad = lax.psum_scatter(
            attn_terms(jnp.int32(0), query_weight.shape[1] * lax.axis_size(("ctx", "fsdp"))),
            ("ctx", "fsdp"),
            scatter_dimension=0,
            tiled=True,
        )
        through_one, gain_one = norm_back(state_in, scale_one, gain_attn, dnormed_one)
        grad = grad_one + through_one
        gain_terms[layer_index] = jnp.stack([gain_one, gain_two], 1)
        grad_parts[layer_index] = (
            attn_grad[:, :D],
            attn_grad[:, D : D + kv_width],
            attn_grad[:, D + kv_width : D + 2 * kv_width],
            attn_grad[:, D + 2 * kv_width :],
            mlp_grad[:, :D],
            mlp_grad[:, D : 2 * D],
            mlp_grad[:, 2 * D :],
        )
    gains_grad = lax.psum_scatter(
        jnp.stack(gain_terms, 0), ("ctx", "fsdp"), scatter_dimension=1, tiled=True
    )
    grads = [jnp.stack([grad_parts[0][kind]], 0) for kind in range(7)] + [gains_grad]
    outputs = [hidden_out[None], grad[None]]
    for kind in range(8):
        update, momentum, variance = adam_step(
            weights[kind], firsts[kind], seconds[kind], grads[kind], RATES[kind], DECAYS[kind]
        )
        outputs.extend([grads[kind], update, momentum, variance])
    return tuple(outputs)


def solution(mesh):
    placed = (
        P("fsdp", "ctx", None),
        P("fsdp", "ctx", None),
        P("fsdp", None),
        P("fsdp", "ctx"),
        P(None, ("ctx", "fsdp"), None),
        P(None, ("ctx", "fsdp"), None),
        P(None, ("ctx", "fsdp"), None),
        P(None, ("ctx", "fsdp"), None),
        P(None, ("ctx", "fsdp"), None),
        P(None, ("ctx", "fsdp"), None),
        P(None, ("ctx", "fsdp"), None),
        P(None, ("ctx", "fsdp"), None),
        P(None, ("ctx", "fsdp"), None),
        P(None, ("ctx", "fsdp"), None),
        P(None, ("ctx", "fsdp"), None),
        P(None, ("ctx", "fsdp"), None),
        P(None, ("ctx", "fsdp"), None),
        P(None, ("ctx", "fsdp"), None),
        P(None, ("ctx", "fsdp"), None),
        P(None, ("ctx", "fsdp"), None),
        P(None, ("ctx", "fsdp"), None),
        P(None, ("ctx", "fsdp"), None),
        P(None, ("ctx", "fsdp"), None),
        P(None, ("ctx", "fsdp"), None),
        P(None, ("ctx", "fsdp"), None),
        P(None, ("ctx", "fsdp"), None),
        P(None, ("ctx", "fsdp"), None),
        P(None, ("ctx", "fsdp"), None),
    )
    return jax.shard_map(
        body,
        mesh=mesh,
        in_specs=placed,
        out_specs=(
            P("fsdp", "ctx", None),
            P("fsdp", "ctx", None),
            P(None, ("ctx", "fsdp"), None),
            P(None, ("ctx", "fsdp"), None),
            P(None, ("ctx", "fsdp"), None),
            P(None, ("ctx", "fsdp"), None),
            P(None, ("ctx", "fsdp"), None),
            P(None, ("ctx", "fsdp"), None),
            P(None, ("ctx", "fsdp"), None),
            P(None, ("ctx", "fsdp"), None),
            P(None, ("ctx", "fsdp"), None),
            P(None, ("ctx", "fsdp"), None),
            P(None, ("ctx", "fsdp"), None),
            P(None, ("ctx", "fsdp"), None),
            P(None, ("ctx", "fsdp"), None),
            P(None, ("ctx", "fsdp"), None),
            P(None, ("ctx", "fsdp"), None),
            P(None, ("ctx", "fsdp"), None),
            P(None, ("ctx", "fsdp"), None),
            P(None, ("ctx", "fsdp"), None),
            P(None, ("ctx", "fsdp"), None),
            P(None, ("ctx", "fsdp"), None),
            P(None, ("ctx", "fsdp"), None),
            P(None, ("ctx", "fsdp"), None),
            P(None, ("ctx", "fsdp"), None),
            P(None, ("ctx", "fsdp"), None),
            P(None, ("ctx", "fsdp"), None),
            P(None, ("ctx", "fsdp"), None),
            P(None, ("ctx", "fsdp"), None),
            P(None, ("ctx", "fsdp"), None),
            P(None, ("ctx", "fsdp"), None),
            P(None, ("ctx", "fsdp"), None),
            P(None, ("ctx", "fsdp"), None),
            P(None, ("ctx", "fsdp"), None),
        ),
        check_vma=False,
    )
```

profile of v0, /device:TPU:0, one launch (start us, length us, event | category | flops | bytes accessed | tf_op | source)
XLA Modules:
  0.0 3945.9 jit_solution(11337727993126799922)
XLA Ops:
  13.3 2.0 convert_element_type.215
  15.4 2.0 convert_element_type.212
  17.4 2.0 convert_element_type.210
  20.3 181.6 %all-gather = bf16[1,2048,2]{2,0,1:T(2,128)(2,1)S(1)} all-gather(bf16[1,16,2]{2,0,1:T(2,128)(2,1)S(1)} %copy.198), channel_id=2, replica_groups=mesh['ctx'=8,'fsdp'=16] {'ctx','fsdp'}, dimensions={1}, use_global_device_ids=true | all-gather | bytes 8256 | tf_op jit(solution)/shard_map/all_gather | solution.py:70
  206.3 1.8 convolution_convert_fusion
  208.1 29.1 all_gather.41
  237.4 157.8 %all-gather.18.cloned.1.call-done = bf16[1,2048,256]{2,1,0:T(8,128)(2,1)} async-done(((bf16[1,16,256]{2,1,0:T(8,128)(2,1)}), bf16[1,2048,256]{2,1,0:T(8,128)(2,1)}) %all-gather.18.cloned.1.call-update) | async-done | bytes 1048592 | tf_op jit(solution)/shard_map/all_gather | solution.py:67
  398.3 25.6 all_gather.43
  423.9 175.5 %all-gather.20.cloned.1.call-done = bf16[1,2048,2048]{2,1,0:T(8,128)(2,1)} async-done(((bf16[1,16,2048]{2,1,0:T(8,128)(2,1)}), bf16[1,2048,2048]{2,1,0:T(8,128)(2,1)}) %all-gather.20.cloned.1.call-update) | async-done | bytes 8388624 | tf_op jit(solution)/shard_map/all_gather | solution.py:66
  599.4 12.4 copy.202
  611.8 5.9 fusion.98
  617.9 7.1 fusion.125
  625.0 8.3 fusion.15
  633.4 8.4 fusion.126
  641.8 161.3 %all-gather.22.cloned.1.call-done = bf16[1,2048,2048]{2,1,0:T(8,128)(2,1)} async-done(((bf16[1,16,2048]{2,1,0:T(8,128)(2,1)}), bf16[1,2048,2048]{2,1,0:T(8,128)(2,1)}) %all-gather.22.cloned.1.call-update) | async-done | bytes 8388624 | tf_op jit(solution)/shard_map/all_gather | solution.py:69
  803.1 4.7 multiply_reduce_fusion.3
  808.0 256.1 %all-gather.28.cloned.1.call-done = bf16[1,5632,2048]{2,0,1:T(2,128)(2,1)} async-done(((bf16[1,44,2048]{2,0,1:T(2,128)(2,1)}), bf16[1,5632,2048]{2,0,1:T(2,128)(2,1)}) %all-gather.28.cloned.1.call-update) | async-done | bytes 23068688 | tf_op jit(solution)/shard_map/all_gather | solution.py:80
  1064.1 21.2 fusion
  1085.3 240.5 %all-gather.26.cloned.1.call-done = bf16[1,5632,2048]{2,0,1:T(2,128)(2,1)} async-done(((bf16[1,44,2048]{2,0,1:T(2,128)(2,1)}), bf16[1,5632,2048]{2,0,1:T(2,128)(2,1)}) %all-gather.26.cloned.1.call-update) | async-done | bytes 23068688 | tf_op jit(solution)/shard_map/all_gather | solution.py:79
  1325.8 21.0 fusion.6
  1346.8 240.2 %all-gather.24.cloned.1.call-done = bf16[1,5632,2048]{2,0,1:T(2,128)(2,1)} async-done(((bf16[1,44,2048]{2,0,1:T(2,128)(2,1)}), bf16[1,5632,2048]{2,0,1:T(2,128)(2,1)}) %all-gather.24.cloned.1.call-update) | async-done | bytes 23068688 | tf_op jit(solution)/shard_map/all_gather | solution.py:78
  1587.0 34.1 multiply_convert_fusion.1
  1621.1 19.2 fusion.129
  1640.3 17.9 fusion.128
  1658.2 28.2 fusion.4
  1686.4 29.1 multiply_reduce_fusion
  1718.1 6.3 fusion.43
  1726.1 8.2 fusion.14
  1734.3 3.3 copy-done
  1737.6 2.6 fusion.65
  1741.3 18.1 fusion.92
  1759.4 8.5 fusion.62
  1769.0 5.0 fusion.127
  1774.3 6.3 fusion.29
  1783.1 34.0 reduce-scatter.16.cloned.1.call-done
  1817.0 3.6 fusion.72
  1820.6 1.9 copy.248
  1822.6 93.1 %pad_maximum_fusion = f32[5632,6144]{0,1:T(8,128)} fusion(f32[5632,2048]{0,1:T(8,128)} %fusion.92, f32[5632,2048]{0,1:T(8,128)} %fusion.129, f32[5632,2048]{0,1:T(8,128)} %fusion.128), kind=kLoop, calls=%fused_computation | loop fusion | flops 69206016 | bytes 276824064 | tf_op jit(solution)/shard_map/concatenate | solution.py:279
  1917.1 8.1 fusion.95
  1925.3 9.2 fusion.85
  1934.5 24.7 pad_maximum_fusion.1
  1962.9 2.2 copy.212
  1965.0 2.2 copy.217
  1967.2 2.1 copy.218
  1969.3 2.2 copy.214
  1971.5 2.2 copy.213
  1973.7 2.2 copy.210
  1975.8 2.2 copy.209
  1978.0 28.3 fusion.49
  2006.3 2.6 fusion.71
  2008.9 451.7 %reduce-scatter.18.cloned.1.call-done = f32[16,2]{1,0:T(8,128)} async-done(((f32[2048,2]{1,0:T(8,128)}), f32[16,2]{1,0:T(8,128)}) %reduce-scatter.18.cloned.1.call-update) | async-done | bytes 144
  2462.0 769.1 %all-reduce.3.cloned.1.call-done = f32[5632,6144]{0,1:T(8,128)} async-done(((f32[5632,6144]{0,1:T(8,128)}), f32[5632,6144]{0,1:T(8,128)}) %all-reduce.3.cloned.1.call-update) | async-done | bytes 138412048
  3231.0 5.1 dynamic-slice_bitcast_fusion.1
  3237.3 9.7 multiply_subtract_fusion
  3247.0 2.1 copy.222
  3249.1 2.1 copy.223
  3251.2 2.1 copy.224
  3253.3 2.1 copy.225
  3255.5 2.1 copy.226
  3257.6 2.1 copy.227
  3259.7 2.1 copy.228
  3261.8 2.1 copy.229
  3267.4 664.7 %reduce-scatter.12.cloned.1.call-done = f32[16,4608]{1,0:T(8,128)} async-done(((f32[2048,4608]{1,0:T(8,128)}), f32[16,4608]{1,0:T(8,128)}) %reduce-scatter.12.cloned.1.call-update) | async-done | bytes 294928 | tf_op jit(solution)/shard_map/reduce_scatter | solution.py:365
  3935.1 2.2 multiply_subtract_fusion.3
  (155 shorter events, 39.7 us)
Async XLA Ops:
  7.2 604.6 %copy-start.1 = (bf16[1,128,2048]{2,1,0:T(8,128)(2,1)S(1)}, bf16[1,128,2048]{2,1,0:T(8,128)(2,1)}, u32[]{:S(2)}) copy-start(bf16[1,128,2048]{2,1,0:T(8,128)(2,1)} %param.28) | copy-start | bytes 1572868
  7.2 199.1 %all-gather.16.cloned.1.call-start = ((), (), s32[]{:S(2)}) async-start(), calls=%async_computation.5 | async-start | bytes 1056768 | tf_op jit(solution)/shard_map/all_gather | solution.py:68
  8.7 386.5 %all-gather.18.cloned.1.call-start = ((), (), s32[]{:S(2)}) async-start(), calls=%async_computation.6 | async-start | bytes 1056768 | tf_op jit(solution)/shard_map/all_gather | solution.py:67
  10.1 589.4 %all-gather.20.cloned.1.call-start = ((), (), s32[]{:S(2)}) async-start(), calls=%async_computation.7 | async-start | bytes 8454144 | tf_op jit(solution)/shard_map/all_gather | solution.py:66
  11.7 791.4 %all-gather.22.cloned.1.call-start = ((), (), s32[]{:S(2)}) async-start(), calls=%async_computation.8 | async-start | bytes 8454144 | tf_op jit(solution)/shard_map/all_gather | solution.py:69
  13.3 1050.8 %all-gather.28.cloned.1.call-start = ((), (), s32[]{:S(2)}) async-start(), calls=%async_computation.11 | async-start | bytes 46497792 | tf_op jit(solution)/shard_map/all_gather | solution.py:80
  15.3 1310.5 %all-gather.26.cloned.1.call-start = ((), (), s32[]{:S(2)}) async-start(), calls=%async_computation.10 | async-start | bytes 46497792 | tf_op jit(solution)/shard_map/all_gather | solution.py:79
  17.4 1569.6 %all-gather.24.cloned.1.call-start = ((), (), s32[]{:S(2)}) async-start(), calls=%async_computation.9 | async-start | bytes 46497792 | tf_op jit(solution)/shard_map/all_gather | solution.py:78
  19.4 1761.2 %reduce-scatter.14.cloned.1.call-start = ((), (), s32[]{:S(2)}) async-start(), calls=%async_computation.12 | async-start | bytes 589824
  204.6 413.1 %copy-start.31 = (f32[128]{0:T(128)}, f32[128]{0:T(128)S(1)}, u32[]{:S(2)}) copy-start(f32[128]{0:T(128)S(1)} %add_rsqrt_fusion.1) | copy-start | bytes 1540
  206.0 411.7 %copy-start.23 = (f32[128,32]{0,1:T(8,128)}, f32[128,32]{0,1:T(8,128)S(1)}, u32[]{:S(2)}) copy-start(f32[128,32]{0,1:T(8,128)S(1)} %get-tuple-element.266) | copy-start | bytes 49156
  206.3 411.4 %copy-start.26 = (f32[2048,1]{0,1:T(1,128)}, f32[2048,1]{0,1:T(1,128)S(1)}, u32[]{:S(2)}) copy-start(f32[2048,1]{0,1:T(1,128)S(1)} %get-tuple-element.263) | copy-start | bytes 24580
  423.9 201.1 %copy-start.7 = (bf16[1024,256]{0,1:T(8,128)(2,1)}, bf16[1024,256]{0,1:T(8,128)(2,1)S(1)}, u32[]{:S(2)}) copy-start(bf16[1024,256]{0,1:T(8,128)(2,1)S(1)} %all_gather.43) | copy-start | bytes 1572868
  617.9 15.5 copy-start.14
  617.9 15.5 copy-start.16
  641.8 443.5 %copy-start.9 = (bf16[128,4,8,64]{0,3,2,1:T(8,128)(2,1)}, bf16[128,4,8,64]{0,3,2,1:T(8,128)(2,1)S(1)}, u32[]{:S(2)}) copy-start(bf16[128,4,8,64]{0,3,2,1:T(8,128)(2,1)S(1)} %get-tuple-element.269) | copy-start | bytes 1572868
  641.8 422.3 %copy-start.18 = (bf16[1,128,2048]{2,1,0:T(8,128)(2,1)S(1)}, bf16[1,128,2048]{2,1,0:T(8,128)(2,1)}, u32[]{:S(2)}) copy-start(bf16[1,128,2048]{2,1,0:T(8,128)(2,1)} %param.29) | copy-start | bytes 1572868
  807.8 907.7 %copy-start.5 = (f32[128,2048]{1,0:T(8,128)}, f32[128,2048]{1,0:T(8,128)S(1)}, u32[]{:S(2)}) copy-start(f32[128,2048]{1,0:T(8,128)S(1)} %get-tuple-element.272) | copy-start | bytes 3145732
  1621.1 19.2 copy-start.13
  1717.1 1.0 copy-start.3
  1726.0 11.6 copy-start.15
  1726.0 11.6 copy-start.17
  1726.1 15.2 copy-start.12
  1734.3 3.3 copy-start
  1741.2 75.8 %reduce-scatter.16.cloned.1.call-start = ((), (), s32[]{:S(2)}) async-start(), calls=%async_computation.13 | async-start | bytes 589824
  1759.4 9.6 copy-start.8
  1759.4 14.6 copy-start.24
  1759.4 14.6 copy-start.28
  1767.9 13.7 copy-start.11
  1767.9 49.1 %copy-start.2 = (bf16[1,128,2048]{2,1,0:T(8,128)(2,1)S(1)}, bf16[1,128,2048]{2,1,0:T(8,128)(2,1)}, u32[]{:S(2)}) copy-start(bf16[1,128,2048]{2,1,0:T(8,128)(2,1)} %param.28) | copy-start | bytes 1572868
  1767.9 49.1 %copy-start.27 = (f32[2048,1]{0,1:T(1,128)S(1)}, f32[2048,1]{0,1:T(1,128)}, u32[]{:S(2)}) copy-start(f32[2048,1]{0,1:T(1,128)} %copy-done.26) | copy-start | bytes 24580
  1768.0 49.1 %copy-start.32 = (f32[128]{0:T(128)S(1)}, f32[128]{0:T(128)}, u32[]{:S(2)}) copy-start(f32[128]{0:T(128)} %copy-done.31) | copy-start | bytes 1540
  1774.2 686.4 %reduce-scatter.18.cloned.1.call-start = ((), (), s32[]{:S(2)}) async-start(), calls=%async_computation.14 | async-start | bytes 1056768
  1822.5 1408.5 %all-reduce.3.cloned.1.call-start = ((), (), s32[]{:S(2)}) async-start(), calls=%async_computation.15 | async-start | bytes 276824064
  1915.7 1.2 copy-start.4
  1915.7 1.4 copy-start.10
  1915.8 9.4 copy-start.25
  1915.8 2016.3 %reduce-scatter.12.cloned.1.call-start = ((), (), s32[]{:S(2)}) async-start(), calls=%async_computation.4 | async-start | bytes 38043648 | tf_op jit(solution)/shard_map/reduce_scatter | solution.py:365
  1959.3 1.0 copy-start.19
  1959.3 2.3 copy-start.20
  1959.3 18.7 copy-start.6
  1978.0 28.3 copy-start.37
  1978.0 483.4 %copy-start.34 = (f32[1,16,2]{1,2,0:T(2,128)S(1)}, f32[1,16,2]{1,2,0:T(2,128)}, u32[]{:S(2)}) copy-start(f32[1,16,2]{1,2,0:T(2,128)} %param.39) | copy-start | bytes 388
  1978.0 483.4 %copy-start.35 = (f32[1,16,2]{1,2,0:T(2,128)S(1)}, f32[1,16,2]{1,2,0:T(2,128)}, u32[]{:S(2)}) copy-start(f32[1,16,2]{1,2,0:T(2,128)} %param.47) | copy-start | bytes 388
  1978.0 483.4 %copy-start.36 = (f32[1,16,2]{1,2,0:T(2,128)S(1)}, f32[1,16,2]{1,2,0:T(2,128)}, u32[]{:S(2)}) copy-start(f32[1,16,2]{1,2,0:T(2,128)} %param.55) | copy-start | bytes 388
  2461.4 0.6 copy-start.33
  3237.3 697.8 %copy-start.21 = (f32[1,16,2048]{2,1,0:T(8,128)S(1)}, f32[1,16,2048]{2,1,0:T(8,128)}, u32[]{:S(2)}) copy-start(f32[1,16,2048]{2,1,0:T(8,128)} %param.32) | copy-start | bytes 393220
  3237.3 697.8 %copy-start.22 = (f32[1,16,2048]{2,1,0:T(8,128)S(1)}, f32[1,16,2048]{2,1,0:T(8,128)}, u32[]{:S(2)}) copy-start(f32[1,16,2048]{2,1,0:T(8,128)} %param.35) | copy-start | bytes 393220
  3237.3 697.8 %copy-start.29 = (f32[1,16,2048]{2,1,0:T(8,128)S(1)}, f32[1,16,2048]{2,1,0:T(8,128)}, u32[]{:S(2)}) copy-start(f32[1,16,2048]{2,1,0:T(8,128)} %param.43) | copy-start | bytes 393220
  3237.3 699.9 %copy-start.30 = (f32[1,16,256]{2,1,0:T(8,128)S(1)}, f32[1,16,256]{2,1,0:T(8,128)}, u32[]{:S(2)}) copy-start(f32[1,16,256]{2,1,0:T(8,128)} %param.34) | copy-start | bytes 49156
Sparse Core Ops, SparseCore 0:
  10.4 193.3 all-gather.15
  206.1 189.0 all-gather.17
  397.5 201.8 all-gather.19
  601.6 201.4 all-gather.21
  805.2 258.8 all-gather.27
  1066.3 259.4 all-gather.25
  1328.1 258.8 all-gather.23
  1741.4 36.6 reduce-scatter.13
  1780.6 36.4 reduce-scatter.15
  1822.7 637.8 reduce-scatter.17
  2467.7 763.3 all-reduce.2
  3233.5 698.5 reduce-scatter.11
where the time goes:
time: 3950 us
  waiting for transfers between devices  3150 us (80%)
  matrix products  306 us (8%)
  blocking collectives  236 us (6%)
  other arithmetic  162 us (4%)
  local copies, waits for them, and re-layouts  74.8 us (2%)
    unnamed x16, waiting for transfers between devices  1250 us
    reduce_scatter x1, waiting for transfers between devices, body(): lax.psum_scatter(attn_terms(jnp.int32(0), query_weight.shape[1] * lax.axi...  665 us
    all_gather x1, waiting for transfers between devices, mlp_fold(): lax.all_gather(pieces[2], ('ctx', 'fsdp'), axis=0, tiled=True)  256 us
    all_gather x1, waiting for transfers between devices, mlp_fold(): lax.all_gather(pieces[1], ('ctx', 'fsdp'), axis=0, tiled=True)  241 us
    all_gather x1, waiting for transfers between devices, mlp_fold(): lax.all_gather(pieces[0], ('ctx', 'fsdp'), axis=0, tiled=True)  240 us
    all_gather x1, blocking collectives, attention_weights(): lax.all_gather(pieces[4], ('ctx', 'fsdp'), axis=0, tiled=True)  182 us
    all_gather x1, waiting for transfers between devices, attention_weights(): lax.all_gather(pieces[0], ('ctx', 'fsdp'), axis=0, tiled=True)  176 us
    all_gather x1, waiting for transfers between devices, attention_weights(): lax.all_gather(pieces[3], ('ctx', 'fsdp'), axis=0, tiled=True)  161 us
  transfers between devices with their start and end apart: 12, of which 10 were waited for; matrix products, arithmetic and copies ran while one was open for 9% of the time, Pallas kernels for 0%

commit v1 on v0

v1 whole, which is shorter than its diff:
```python
import functools
import math

import jax
import jax.numpy as jnp
from jax import lax
from jax.experimental import pallas as pl
from jax.experimental.pallas import tpu as pltpu
from jax.sharding import PartitionSpec as P

D = 2048
HEADS = 32
KV_HEADS = 4
HEAD = 64
FF = 5632
STEP = 10
N_CTX = 8
N_X = 4
MINE = HEADS // N_X
WIDE = MINE * HEAD
PACK = WIDE + 2 * HEAD
UNITS = 44
PADDED = 48

EPS = 1e-05
NEG = -1e30
BETA_ONE = 0.9
BETA_TWO = 0.95
ADAM_EPS = 1e-08
RATES = (0.1, 0.1, 0.1, 1.5, 0.1, 0.1, 0.066, 0.5)
DECAYS = (0.1, 0.1, 0.1, 0.1, 0.1, 0.1, 0.1, 0.0)
BY_COLUMN = (((1,), (1,)), ((), ()))
BY_ROW = (((0,), (0,)), ((), ()))
bf16 = jnp.bfloat16
f32 = jnp.float32

AXES = ("x", "zl", "zh", "y", "core")
SHARE = ("zh", "zl", "y")
SWAP = [(0, 1), (1, 0)]
RING_X = ("x", [(i, (i + 1) % 4) for i in range(4)], [(i, (i - 1) % 4) for i in range(4)])
RING_Y = ("y",) + RING_X[1:]
DEPTH = (0, 2, 1, 3)
RING_Z = (
    ("zl", "zh"),
    [(DEPTH[i], DEPTH[(i + 1) % 4]) for i in range(4)],
    [(DEPTH[i], DEPTH[(i - 1) % 4]) for i in range(4)],
)
STEPS = (0, -1, 1, 2)


def across(ring):
    there = dict(ring[1])
    return [(i, there[there[i]]) for i in there]


def after(value, *others):
    return lax.optimization_barrier((value,) + others)[0]


def add(*terms):
    total = terms[0].astype(f32)
    for term in terms[1:]:
        total = total + term.astype(f32)
    return total


def place(blocks, spots, axis):
    shape = list(blocks[0].shape)
    shape.insert(axis, len(blocks))
    whole = jnp.zeros(shape, blocks[0].dtype)
    for block, spot in zip(blocks, spots):
        at = [0] * len(shape)
        at[axis] = spot
        whole = lax.dynamic_update_slice(whole, jnp.expand_dims(block, axis), tuple(at))
    return whole


def ring_halves(block, ring):
    name, right, left = ring
    half = block.shape[0] // 2
    from_left = lax.ppermute(block, name, right)
    from_right = lax.ppermute(block, name, left)
    first = lax.ppermute(from_left[:half], name, right)
    second = lax.ppermute(from_right[half:], name, left)
    return [block, from_left, from_right, first, second]


def ring_small(block, ring):
    name, right, left = ring
    return [
        block,
        lax.ppermute(block, name, right),
        lax.ppermute(block, name, left),
        lax.ppermute(block, name, across(ring)),
    ]


def ring_sum_small(own, to_left, to_right, far, ring):
    name, right, left = ring
    return add(
        own,
        lax.ppermute(to_left, name, left),
        lax.ppermute(to_right, name, right),
        lax.ppermute(far, name, across(ring)),
    )


def gather_x_core(block):
    blocks = ring_halves(block, RING_X)
    return blocks + [lax.ppermute(b, "core", SWAP) for b in blocks]


def ring_spots():
    at = lax.axis_index("x"), lax.axis_index("y")
    side, far_side, core = (lax.axis_index(n) for n in ("zl", "zh", "core"))
    spots_x, spots_y = ([(a + step) % 4 for step in STEPS] for a in at)
    depth = [(far_side * 2 + side + step) % 4 for step in STEPS]
    spots_z = [d % 2 * 2 + d // 2 for d in depth]
    return spots_x, spots_y, spots_z, [core, 1 - core]


def pick(value, spot, axis):
    return lax.dynamic_index_in_dim(value, spot, axis, False)


def rope_tables(places):
    half = HEAD // 2
    freqs = jnp.exp(jnp.arange(half, dtype=f32) * (-2.0 * math.log(10000.0) / HEAD))
    angles = places.astype(f32)[:, None] * freqs[None, :]
    return jnp.cos(angles), jnp.sin(angles)


def dot(left, right, dims, kind):
    return lax.dot_general(left, right, dims, preferred_element_type=f32).astype(kind)


def adam_step(weight, first, second, grad, rate, decay):
    momentum = BETA_ONE * first + (1.0 - BETA_ONE) * grad
    variance = BETA_TWO * second + (1.0 - BETA_TWO) * grad * grad
    corrected = momentum / (1.0 - BETA_ONE**STEP)
    root = jnp.sqrt(variance / (1.0 - BETA_TWO**STEP))
    update = weight - rate * (corrected / (root + ADAM_EPS) + decay * weight)
    return (update, momentum, variance)


def call(kernel, outs, ins, scratch=(), prefetch=(), flops=0, traffic=0):
    spec_any = pl.BlockSpec(memory_space=pl.ANY)
    spec_vmem = pl.BlockSpec(memory_space=pltpu.VMEM)
    spec_smem = pl.BlockSpec(memory_space=pltpu.SMEM)
    return pl.pallas_call(
        kernel,
        out_shape=[jax.ShapeDtypeStruct(shape, kind) for shape, kind in outs],
        in_specs=[spec_smem] * len(prefetch)
        + [spec_vmem if inside else spec_any for _, inside in ins],
        out_specs=[spec_vmem] * len(outs),
        scratch_shapes=list(scratch),
        compiler_params=pltpu.CompilerParams(vmem_limit_bytes=56 * 1024 * 1024),
        cost_estimate=pl.CostEstimate(flops=flops, bytes_accessed=traffic, transcendentals=0),
    )(*prefetch, *(array for array, _ in ins))


def matmul(left, right, dims=(((1,), (0,)), ((), ()))):
    return lax.dot_general(left, right, dims, preferred_element_type=f32)


def lanes(shape):
    return lax.broadcasted_iota(jnp.int32, shape, 1)


def prepare_kernel(state_ref, table_ref, out_ref):
    value = state_ref[...].astype(f32)
    scale = lax.rsqrt(jnp.mean(value * value, -1, keepdims=True) + EPS)
    out_ref[:, :D] = (value * scale).astype(bf16)
    out_ref[:, D:] = table_ref[...]


def join_kernel(*refs):
    at = 0
    for ref in refs[:-1]:
        refs[-1][at : at + ref.shape[0], :] = ref[...]
        at += ref.shape[0]


def join(blocks):
    shape = (sum(b.shape[0] for b in blocks), blocks[0].shape[1])
    return call(join_kernel, [(shape, blocks[0].dtype)], [(b, True) for b in blocks])[0]


def output_kernel(res_ref, own, left, right, low, high, out_ref):
    for at, part in zip((0, 64), sum_arrived(own, left, right, low, high)):
        rows = slice(at, at + 64)
        out_ref[rows, :] = (res_ref[rows, :] + part).astype(bf16)


def swap_halves(value):
    low = lanes(value.shape) % HEAD < HEAD // 2
    return jnp.where(low, pltpu.roll(value, 96, 1), pltpu.roll(value, 32, 1))


def rope_factors(angles):
    low = lanes(angles.shape) % HEAD < HEAD // 2
    cosine = jnp.where(low, angles, pltpu.roll(angles, 32, 1))
    sine = jnp.where(low, -pltpu.roll(angles, 96, 1), angles)
    return cosine, sine


PIECES = (128, 128, 128, 64, 64)


def starts(sizes):
    at, found = 0, []
    for size in sizes:
        found.append(at)
        at += size
    return found


def project_kernel(spots, *refs):
    tokens, weights = refs[:5], refs[5:13]
    query_ref, pair_ref, normed_ref, full_ref, gain_ref, angle_ref = refs[13:19]
    table_buf, weight_buf, sems = refs[19:]
    copies = []
    for i, (at, size) in enumerate(zip(starts(PIECES), PIECES)):
        rows = pl.ds(at, size)
        copies.append(
            pltpu.make_async_copy(tokens[i].at[:, pl.ds(0, D)], normed_ref.at[rows], sems.at[2 * i])
        )
        copies.append(
            pltpu.make_async_copy(
                tokens[i].at[:, pl.ds(D, 128)], table_buf.at[rows], sems.at[2 * i + 1]
            )
        )
    for i in range(8):
        copies.append(
            pltpu.make_async_copy(
                weights[i], weight_buf.at[i // 4, pl.ds(i % 4 * 256, 256)], sems.at[10 + i]
            )
        )
    for copy in copies:
        copy.start()
    for copy in copies:
        copy.wait()
    for side in range(2):
        for deep in range(4):
            for up in range(4):
                for along in range(4):
                    at = deep * 256 + up * 64 + along * 16
                    block = weight_buf[side, at : at + 16, :]
                    to = spots[along] * 4 + spots[8 + deep]
                    to = ((to * 4 + spots[4 + up]) * 2 + spots[12 + side]) * 16
                    to = pl.multiple_of(to, 16)
                    full_ref[pl.ds(to, 16), :] = block[:, :PACK]
                    gain_ref[pl.ds(to, 16), :] = block[:, PACK:]
    table = table_buf[...].astype(f32)
    angles = table + pltpu.roll(table, 64, 1)
    angle_ref[...] = angles
    for at in range(0, 512, 256):
        rows = slice(at, at + 256)
        cosine, sine = rope_factors(angles[rows])
        for col in range(0, PACK, 128):
            part = matmul(normed_ref[rows, :], full_ref[:, col : col + 128])
            turned = part * cosine + swap_halves(part) * sine
            if col < WIDE:
                query_ref[rows, col : col + 128] = (turned * HEAD**-0.5).astype(bf16)
            else:
                turned = jnp.where(lanes(part.shape) < HEAD, turned, part)
                pair_ref[rows, :] = turned.astype(bf16)


def attend_kernel(spots, *refs):
    query_ref, own_ref, other_ref, row_ref, column_ref = refs[:5]
    weights = refs[5:13]
    mixed_ref, sum_ref, full_ref, own_out, left_out, right_out, low_out, high_out = refs[13:21]
    weight_buf, key_buf, value_buf, sems = refs[21:]
    copies = []
    for i in range(8):
        copies.append(
            pltpu.make_async_copy(
                weights[i], weight_buf.at[i // 4, pl.ds(i % 4 * 64, 64)], sems.at[i]
            )
        )
    for copy in copies:
        copy.start()
    split_pairs(own_ref, other_ref, key_buf, value_buf)
    visible = column_ref[...] <= row_ref[...]
    logs = jnp.zeros((512, 128), f32)
    for pair in range(MINE // 2):
        cols = slice(pair * 128, pair * 128 + 128)
        both = query_ref[:, cols]
        mixed = jnp.zeros((512, 128), f32)
        for side in range(2):
            scores = matmul(both, key_buf[side], BY_COLUMN)
            scores = jnp.where(visible, scores, NEG)
            peak = jnp.max(scores, -1, keepdims=True)
            expo = jnp.exp(scores - peak)
            total = jnp.sum(expo, -1, keepdims=True)
            probs = (expo * (1.0 / total)).astype(bf16)
            mixed = mixed + matmul(probs, value_buf[side])
            logs = jnp.where(
                lanes(logs.shape) == pair * 2 + side, peak + jnp.log(total), logs
            )
        mixed_ref[:, cols] = mixed.astype(bf16)
    sum_ref[...] = logs
    for copy in copies:
        copy.wait()
    for side in range(2):
        for deep in range(4):
            for up in range(4):
                at = deep * 64 + up * 16
                to = (spots[8 + deep] * 4 + spots[4 + up]) * 2 + spots[12 + side]
                to = pl.multiple_of(to * 16, 16)
                full_ref[pl.ds(to, 16), :] = weight_buf[side, at : at + 16, :]
    put_parts(
        lambda at, size: matmul(mixed_ref[at : at + size, :], full_ref[...]).astype(bf16),
        (own_out, left_out, right_out, low_out, high_out),
    )


def split_pairs(own_ref, other_ref, key_buf, value_buf):
    for i, ref in enumerate((own_ref, other_ref)):
        rows = slice(i * 512, i * 512 + 512)
        pair = ref[...].astype(f32)
        low = lanes(pair.shape) < HEAD
        key, value = jnp.where(low, pair, 0.0), jnp.where(low, 0.0, pair)
        key_buf[0, rows, :] = key.astype(bf16)
        key_buf[1, rows, :] = pltpu.roll(key, HEAD, 1).astype(bf16)
        value_buf[0, rows, :] = pltpu.roll(value, HEAD, 1).astype(bf16)
        value_buf[1, rows, :] = value.astype(bf16)


def put_parts(rows_at, outs):
    own, left, right, low, high = outs
    value = rows_at(0, 256)
    own[...] = value[:128]
    low[...] = value[128:192]
    left[64:, :] = value[192:]
    value = rows_at(256, 256)
    right[64:, :] = value[:64]
    high[...] = value[64:128]
    left[:64, :] = value[128:192]
    right[:64, :] = value[192:]


def put_both(rows_at, outs):
    first, second = outs[5:]
    put_parts(rows_at, outs[:5])
    put_parts(
        lambda at, size: rows_at(512 + at, size),
        (
            second.at[pl.ds(0, 128)],
            first.at[pl.ds(0, 128)],
            first.at[pl.ds(128, 128)],
            second.at[pl.ds(128, 64)],
            second.at[pl.ds(192, 64)],
        ),
    )


PARTS = (((128, D), bf16), ((128, D), bf16), ((128, D), bf16), ((64, D), bf16), ((64, D), bf16))


def scatter_parts(parts):
    own, left, right, low, high = parts
    name, to_right, to_left = RING_X
    got_left = lax.ppermute(left, name, to_left)
    got_right = lax.ppermute(right, name, to_right)
    low = add(low, got_left[:64]).astype(bf16)
    high = add(high, got_right[:64]).astype(bf16)
    return own, got_left, got_right, lax.ppermute(low, name, to_left), lax.ppermute(high, name, to_right)


BOTH_PARTS = PARTS + (((256, D), bf16), ((256, D), bf16))


def scatter_both(parts):
    own, left, right, low, high, first, second = parts
    first = lax.ppermute(first, "core", SWAP)
    second = lax.ppermute(second, "core", SWAP)
    left = add(left, first[:128]).astype(bf16)
    right = add(right, first[128:]).astype(bf16)
    own = add(own, second[:128]).astype(bf16)
    low = add(low, second[128:192]).astype(bf16)
    high = add(high, second[192:]).astype(bf16)
    return scatter_parts((own, left, right, low, high))


def sum_arrived(own, got_left, got_right, low, high):
    first = own[:64, :].astype(f32) + got_right[64:, :].astype(f32) + low[...].astype(f32)
    second = own[64:, :].astype(f32) + got_left[64:, :].astype(f32) + high[...].astype(f32)
    return first, second


def residual_kernel(state_ref, gain_ref, own, left, right, low, high, out_ref, rows_ref):
    for at, part in zip((0, 64), sum_arrived(own, left, right, low, high)):
        rows = slice(at, at + 64)
        value = state_ref[rows, :].astype(f32) + part
        out_ref[rows, :] = value
        scale = lax.rsqrt(jnp.mean(value * value, -1, keepdims=True) + EPS)
        rows_ref[rows, :] = (value * scale * gain_ref[...]).astype(bf16)


def back_two_kernel(grad_ref, gain_ref, res_ref, own, left, right, low, high, out_ref, low_ref, term_ref):
    terms = jnp.zeros((1, D), f32)
    for at, part in zip((0, 64), sum_arrived(own, left, right, low, high)):
        rows = slice(at, at + 64)
        value = res_ref[rows, :]
        scale = lax.rsqrt(jnp.mean(value * value, -1, keepdims=True) + EPS)
        normed = value * scale
        terms = terms + jnp.sum(part * normed, 0, keepdims=True)
        weighted = part * gain_ref[...]
        through = scale * (weighted - normed * jnp.mean(weighted * normed, -1, keepdims=True))
        total = grad_ref[rows, :].astype(f32) + through
        out_ref[rows, :] = total
        low_ref[rows, :] = total.astype(bf16)
    term_ref[...] = terms


def back_one_kernel(grad_ref, state_ref, own, left, right, low, high, out_ref):
    for at, part in zip((0, 64), sum_arrived(own, left, right, low, high)):
        rows = slice(at, at + 64)
        value = state_ref[rows, :].astype(f32)
        scale = lax.rsqrt(jnp.mean(value * value, -1, keepdims=True) + EPS)
        normed = value * scale
        through = scale * (part - normed * jnp.mean(part * normed, -1, keepdims=True))
        out_ref[rows, :] = grad_ref[rows, :] + through


def mlp_kernel(*refs):
    tokens, grads, weight_ref = refs[:10], refs[10:20], refs[20]
    outs = refs[21:28]
    hidden_ref, dgate_ref, dup_ref, rows_ref, grads_ref = refs[28:33]
    weight_buf, sum_buf, sems = refs[33:]
    copies = []
    for kind in range(3):
        copies.append(
            pltpu.make_async_copy(
                weight_ref.at[:, pl.ds(kind * PADDED, PADDED)], weight_buf.at[kind], sems.at[kind]
            )
        )
    for i in range(10):
        at = starts(PIECES + PIECES)[i]
        rows = pl.ds(at, tokens[i].shape[0])
        copies.append(pltpu.make_async_copy(tokens[i], rows_ref.at[rows], sems.at[3 + i]))
        copies.append(pltpu.make_async_copy(grads[i], grads_ref.at[rows], sems.at[13 + i]))
    for copy in copies:
        copy.start()
    for copy in copies:
        copy.wait()

    def step(i, carry):
        rows = pl.ds(pl.multiple_of(i * 256, 256), 256)
        for col in range(0, 768, 384):
            cols = slice(col, col + 384)
            gate_w, up_w, down_w = (
                weight_buf[k, col // PADDED : (col + 384) // PADDED].reshape(384, D)
                for k in range(3)
            )
            gate = matmul(rows_ref[rows, :], gate_w, BY_COLUMN)
            up_proj = matmul(rows_ref[rows, :], up_w, BY_COLUMN)
            dhidden = matmul(grads_ref[rows, :], down_w, BY_COLUMN)
            sigmoid = 1.0 / (1.0 + jnp.exp(-gate))
            silu_gate = gate * sigmoid
            hidden_ref[rows, cols] = (silu_gate * up_proj).astype(bf16)
            slope = sigmoid * (1.0 + gate * (1.0 - sigmoid))
            dgate_ref[rows, cols] = (dhidden * up_proj * slope).astype(bf16)
            dup_ref[rows, cols] = (dhidden * silu_gate).astype(bf16)
        summed = matmul(dgate_ref[rows, :], weight_buf[0].reshape(768, D))
        summed = summed + matmul(dup_ref[rows, :], weight_buf[1].reshape(768, D))
        sum_buf[rows, :] = summed.astype(bf16)
        return carry

    lax.fori_loop(0, 4, step, 0)
    put_both(lambda at, size: sum_buf[at : at + size, :], outs)


def mlp_grad_kernel(left_ref, right_ref, *refs):
    out_ref = refs[-1]
    terms = matmul(left_ref[...], right_ref[...], BY_ROW).astype(bf16)
    out_ref[...] = terms.reshape(16, PADDED, terms.shape[1])


def mlp_grad(kind, left, right, before):
    width = 512
    held = [] if before is None else [before]
    return pl.pallas_call(
        mlp_grad_kernel,
        grid=(D // width,),
        out_shape=jax.ShapeDtypeStruct((16, 3 * PADDED, D), bf16),
        in_specs=[
            pl.BlockSpec((1024, 768), lambda i: (0, 0)),
            pl.BlockSpec((1024, width), lambda i: (0, i)),
        ]
        + [pl.BlockSpec(memory_space=pl.ANY)] * len(held),
        out_specs=pl.BlockSpec((16, PADDED, width), lambda i, kind=kind: (0, kind, i)),
        input_output_aliases={2: 0} if held else {},
        compiler_params=pltpu.CompilerParams(vmem_limit_bytes=40 * 1024 * 1024),
        cost_estimate=pl.CostEstimate(
            flops=2 * 1024 * 768 * D, bytes_accessed=8 * 2**20, transcendentals=0
        ),
    )(left, right, *held)


def branch_kernel(hidden_ref, weight_ref, *refs):
    outs, weight_buf, sem = refs[:7], refs[7], refs[8]
    copy = pltpu.make_async_copy(
        weight_ref.at[:, pl.ds(2 * PADDED, PADDED)], weight_buf, sem.at[0]
    )
    copy.start()
    copy.wait()
    put_both(
        lambda at, size: matmul(
            hidden_ref[at : at + size, :], weight_buf[...].reshape(768, D)
        ).astype(bf16),
        outs,
    )


def unmix_kernel(*refs):
    pieces, full_ref = refs[:5], refs[5]
    joined_ref, dmixed_ref, sems = refs[6:]
    copies = []
    for i, (at, size) in enumerate(zip(starts(PIECES), PIECES)):
        copies.append(pltpu.make_async_copy(pieces[i], joined_ref.at[pl.ds(at, size)], sems.at[i]))
    for copy in copies:
        copy.start()
    for copy in copies:
        copy.wait()
    for at in range(0, 512, 256):
        dmixed_ref[at : at + 256, :] = matmul(
            joined_ref[at : at + 256, :], full_ref[...], BY_COLUMN
        ).astype(bf16)


def attend_back_kernel(pair, query_ref, own_ref, other_ref, row_ref, column_ref, sum_ref, mixed_ref,
                       dmixed_ref, angle_ref, *refs):
    before = refs[0] if pair else None
    dquery_ref, dpair_ref, key_buf, value_buf = refs[1 if pair else 0 :]
    split_pairs(own_ref, other_ref, key_buf, value_buf)
    visible = column_ref[...] <= row_ref[...]
    cols = slice(pair * 128, pair * 128 + 128)
    both, dboth = query_ref[:, cols], dmixed_ref[:, cols]
    product = dboth.astype(f32) * mixed_ref[:, cols].astype(f32)
    low = lanes(product.shape) < HEAD
    dquery = jnp.zeros((512, 128), f32)
    dkeys, dvalues = [], []
    for side in range(2):
        delta = jnp.sum(jnp.where(low == (side == 0), product, 0.0), -1, keepdims=True)
        head = pair * 2 + side
        logs = sum_ref[:, head : head + 1]
        scores = matmul(both, key_buf[side], BY_COLUMN)
        probs = jnp.exp(jnp.where(visible, scores, NEG) - logs)
        dprobs = matmul(dboth, value_buf[side], BY_COLUMN)
        dscores = (probs * (dprobs - delta)).astype(bf16)
        dquery = dquery + matmul(dscores, key_buf[side])
        dkeys.append(matmul(dscores, both, BY_ROW))
        dvalues.append(matmul(probs.astype(bf16), dboth, BY_ROW))
    cosine, sine = rope_factors(angle_ref[...])
    dquery = dquery * HEAD**-0.5
    dquery_ref[...] = (dquery * cosine - swap_halves(dquery) * sine).astype(bf16)
    low = lanes((1024, 128)) < HEAD
    dkey = dkeys[0] + pltpu.roll(dkeys[1], HEAD, 1)
    dvalue = pltpu.roll(dvalues[0], HEAD, 1) + dvalues[1]
    total = jnp.where(low, dkey, dvalue)
    if pair:
        total = total + before[...]
    dpair_ref[...] = total


def finish_kernel(query0, query1, query2, query3, dpair_ref, got_ref, angle_ref, full_ref,
                  proj_ref, own_out, left_out, right_out, low_out, high_out):
    for i, ref in enumerate((query0, query1, query2, query3)):
        proj_ref[:, i * 128 : i * 128 + 128] = ref[...]
    total = dpair_ref[:512, :] + got_ref[...].astype(f32)
    cosine, sine = rope_factors(angle_ref[...])
    turned = total * cosine - swap_halves(total) * sine
    total = jnp.where(lanes(total.shape) < HEAD, turned, total)
    proj_ref[:, WIDE:] = total.astype(bf16)
    put_parts(
        lambda at, size: matmul(proj_ref[at : at + size, :], full_ref[...], BY_COLUMN).astype(bf16),
        (own_out, left_out, right_out, low_out, high_out),
    )


def terms_kernel(normed_ref, proj_ref, gain_ref, out_ref):
    for at in range(0, D, 512):
        rows = slice(at, at + 512)
        out_ref[rows, :PACK] = matmul(normed_ref[:, rows], proj_ref[...], BY_ROW).astype(bf16)
    out_ref[:, PACK:] = gain_ref[...]


def body(
    hidden_in,
    cotangent,
    block_table,
    positions,
    query_weight,
    key_weight,
    value_weight,
    output_weight,
    gate_weight,
    up_weight,
    down_weight,
    norm_gains,
    *moments,
):
    weights = (
        query_weight,
        key_weight,
        value_weight,
        output_weight,
        gate_weight,
        up_weight,
        down_weight,
        norm_gains,
    )
    firsts, seconds = moments[:8], moments[8:]
    tokens = hidden_in.shape[1]
    block_rows = tokens // 2
    spots_x, spots_y, spots_z, spots_core = ring_spots()
    at_side = lax.axis_index("zl")
    places = [spot * 2 + (at_side ^ flip) for flip in range(2) for spot in spots_x]
    table = block_table[0].reshape(N_CTX, 2)[jnp.stack(places)].reshape(-1)
    logical = (
        table[:, None] * block_rows + jnp.arange(block_rows, dtype=jnp.int32)[None, :]
    ).reshape(-1)

    mlp_rows = jnp.concatenate(
        [
            jnp.pad(w[0].astype(bf16), ((0, PADDED - UNITS), (0, 0)))
            for w in (gate_weight, up_weight, down_weight)
        ],
        0,
    )
    mlp_full = lax.all_gather(mlp_rows, SHARE, axis=0, tiled=True)
    mlp_full = mlp_full.reshape(-1, 3 * PADDED, D)

    gains = norm_gains[0].astype(bf16).astype(f32)
    gain_one = gains[:, :1]
    low = [w[0].astype(bf16).astype(f32) for w in (query_weight, key_weight, value_weight)]
    scaled = [(w * gain_one).astype(bf16) for w in low]
    rows = scaled[0].shape[0]
    packed = jnp.concatenate(
        [w.reshape(rows, N_X, -1).transpose(1, 0, 2) for w in scaled]
        + [jnp.broadcast_to(gains[:, 1:].astype(bf16), (N_X, rows, 128))],
        -1,
    )
    name, right, left = RING_X
    owned = join(
        [
            pick(packed, spots_x[0], 0),
            lax.ppermute(pick(packed, spots_x[2], 0), name, right),
            lax.ppermute(pick(packed, spots_x[1], 0), name, left),
            lax.ppermute(pick(packed, spots_x[3], 0), name, across(RING_X)),
        ]
    )
    owned = ring_small(join(ring_small(owned, RING_Y)), RING_Z)
    weight_pieces = owned + [lax.ppermute(b, "core", SWAP) for b in owned]

    state = hidden_in[0]
    tables = jnp.concatenate(rope_tables(positions[0]), 1)
    tables_low = tables.astype(bf16)
    rest = (tables - tables_low.astype(f32)).astype(bf16)
    sent = call(
        prepare_kernel,
        [((tokens, D + 128), bf16)],
        [(state, True), (jnp.concatenate([tables_low, rest], 1), True)],
    )[0]
    token_pieces = ring_halves(sent, RING_X)
    spots = jnp.stack(spots_x + spots_y + spots_z + spots_core).astype(jnp.int32)
    query, own_pair, normed_all, qkv_full, gain_rows, angles = call(
        project_kernel,
        [
            ((512, WIDE), bf16),
            ((512, 128), bf16),
            ((512, D), bf16),
            ((D, PACK), bf16),
            ((D, 128), bf16),
            ((512, 128), f32),
        ],
        [(v, False) for v in token_pieces + weight_pieces],
        scratch=[
            pltpu.VMEM((512, 128), bf16),
            pltpu.VMEM((2, 1024, PACK + 128), bf16),
            pltpu.SemaphoreType.DMA((18,)),
        ],
        prefetch=[spots],
        flops=2 * 512 * D * PACK,
        traffic=12 * 2**20,
    )
    gain_two = gain_rows[:, 0].astype(f32)[None]

    output_low = after(output_weight[0].astype(bf16), owned[3])
    output_low = ring_small(join(ring_small(output_low, RING_Y)), RING_Z)
    output_pieces = output_low + [lax.ppermute(b, "core", SWAP) for b in output_low]
    grad_pieces = gather_x_core(after(cotangent[0], query))

    other_pair = lax.ppermute(own_pair, "zl", SWAP)
    row, column = logical[:512, None], logical[None, :]
    mixed, logs, output_full, *parts = call(
        attend_kernel,
        [((512, WIDE), bf16), ((512, 128), f32), ((WIDE, D), bf16)] + list(PARTS),
        [(v, True) for v in (query, own_pair, other_pair, row, column)]
        + [(v, False) for v in output_pieces],
        scratch=[
            pltpu.VMEM((2, 256, D), bf16),
            pltpu.VMEM((2, 1024, 128), bf16),
            pltpu.VMEM((2, 1024, 128), bf16),
            pltpu.SemaphoreType.DMA((8,)),
        ],
        prefetch=[spots],
        flops=2 * 512 * D * WIDE + 4 * 8 * 512 * 1024 * 256,
        traffic=12 * 2**20,
    )
    residual, mlp_in = call(
        residual_kernel,
        [((tokens, D), f32), ((tokens, D), bf16)],
        [(v, True) for v in (state, gain_two) + scatter_parts(parts)],
    )

    row_pieces = gather_x_core(mlp_in)
    *parts, hidden, dgate, dup, rows_in, grad_rows = call(
        mlp_kernel,
        list(BOTH_PARTS) + [((1024, 768), bf16)] * 3 + [((1024, D), bf16)] * 2,
        [(v, False) for v in row_pieces + grad_pieces + [mlp_full]],
        scratch=[
            pltpu.VMEM((3, 16, PADDED, D), bf16),
            pltpu.VMEM((1024, D), bf16),
            pltpu.SemaphoreType.DMA((23,)),
        ],
        flops=10 * 1024 * 768 * D,
        traffic=30 * 2**20,
    )
    arrived = scatter_both(parts)
    terms = None
    for kind, (over, under) in enumerate(
        ((dgate, rows_in), (dup, rows_in), (hidden, grad_rows))
    ):
        terms = mlp_grad(kind, over, under, terms)
    mlp_terms = lax.psum_scatter(
        terms.reshape(-1, D), SHARE, scatter_dimension=0, tiled=True
    )
    mlp_grads = mlp_terms.astype(f32).reshape(3, PADDED, D)[:, :UNITS]

    grad_one, grad_low, gain_terms = call(
        back_two_kernel,
        [((tokens, D), f32), ((tokens, D), bf16), ((1, D), f32)],
        [(v, True) for v in (cotangent[0], gain_two, residual) + arrived],
    )
    grad_one_pieces = ring_halves(grad_low, RING_X)
    gain_terms = jnp.broadcast_to(gain_terms.reshape(D, 1), (D, 128)).astype(bf16)

    attn_grad, dmixed = call(
        unmix_kernel,
        [((512, D), bf16), ((512, WIDE), bf16)],
        [(v, False) for v in grad_one_pieces] + [(output_full, True)],
        scratch=[pltpu.SemaphoreType.DMA((5,))],
        flops=2 * 512 * D * WIDE,
        traffic=6 * 2**20,
    )
    output_terms = dot(mixed, attn_grad, BY_ROW, bf16).reshape(4, 4, 2, rows, D)
    given = lax.ppermute(pick(output_terms, spots_core[1], 2), "core", SWAP)
    output_terms = add(pick(output_terms, spots_core[0], 2), given).astype(bf16)
    output_terms = ring_sum_small(*(pick(output_terms, spot, 0) for spot in spots_z), RING_Z)
    output_terms = output_terms.astype(bf16)
    output_grad = ring_sum_small(*(pick(output_terms, spot, 0) for spot in spots_y), RING_Y)
    dqueries, dpair = [], None
    for pair in range(MINE // 2):
        dquery, dpair = call(
            functools.partial(attend_back_kernel, pair),
            [((512, 128), bf16), ((1024, 128), f32)],
            [
                (v, True)
                for v in (query, own_pair, other_pair, row, column, logs, mixed, dmixed, angles)
            ]
            + ([(dpair, True)] if pair else []),
            scratch=[pltpu.VMEM((2, 1024, 128), bf16)] * 2,
            flops=10 * 2 * 512 * 1024 * 256,
            traffic=4 * 2**20,
        )
        dqueries.append(dquery)
    got = lax.ppermute(dpair[512:].astype(bf16), "zl", SWAP)
    dprojected, *parts = call(
        finish_kernel,
        [((512, PACK), bf16)] + list(PARTS),
        [(v, True) for v in dqueries + [dpair, got, angles, qkv_full]],
        flops=2 * 512 * D * PACK,
        traffic=8 * 2**20,
    )
    hidden_grad = call(
        back_one_kernel,
        [((tokens, D), f32)],
        [(v, True) for v in (grad_one, state) + scatter_parts(parts)],
    )[0]
    branch = call(
        branch_kernel,
        BOTH_PARTS,
        [(after(hidden, dmixed), True), (mlp_full, False)],
        scratch=[pltpu.VMEM((16, PADDED, D), bf16), pltpu.SemaphoreType.DMA((1,))],
        flops=2 * 1024 * 768 * D,
        traffic=8 * 2**20,
    )
    hidden_out = call(
        output_kernel,
        [((tokens, D), bf16)],
        [(v, True) for v in (residual,) + scatter_both(branch)],
    )[0]

    qkv_terms = call(
        terms_kernel,
        [((D, PACK + 128), bf16)],
        [(v, True) for v in (normed_all, dprojected, gain_terms)],
        flops=2 * 512 * D * PACK,
        traffic=6 * 2**20,
    )[0]
    qkv_terms = qkv_terms.reshape(N_X, 4, 4, 2, rows, -1)
    given = lax.ppermute(pick(qkv_terms, spots_core[1], 3), "core", SWAP)
    qkv_terms = add(pick(qkv_terms, spots_core[0], 3), given).astype(bf16)
    qkv_terms = ring_sum_small(*(pick(qkv_terms, spot, 1) for spot in spots_z), RING_Z)
    qkv_terms = qkv_terms.astype(bf16)
    qkv_terms = ring_sum_small(*(pick(qkv_terms, spot, 1) for spot in spots_y), RING_Y)
    qkv_terms = qkv_terms.astype(bf16)
    qkv_grad = place(
        [
            pick(qkv_terms, spots_x[0], 0),
            lax.ppermute(pick(qkv_terms, spots_x[2], 0), name, right),
            lax.ppermute(pick(qkv_terms, spots_x[1], 0), name, left),
            lax.ppermute(pick(qkv_terms, spots_x[3], 0), name, across(RING_X)),
        ],
        spots_x,
        0,
    ).astype(f32)
    bare = [
        qkv_grad[..., low_end:high_end].transpose(1, 0, 2).reshape(rows, -1)
        for low_end, high_end in ((0, WIDE), (WIDE, WIDE + HEAD), (WIDE + HEAD, PACK))
    ]
    gain_two_grad = jnp.sum(qkv_grad[..., PACK], 0)
    gain_one_grad = sum(jnp.sum(w * b, 1) for w, b in zip(low, bare))
    grads = [b * gain_one for b in bare]
    grads += [output_grad, mlp_grads[0], mlp_grads[1], mlp_grads[2]]
    grads.append(jnp.stack([gain_one_grad, gain_two_grad], 1))

    outputs = [hidden_out[None], hidden_grad[None]]
    for kind in range(8):
        full = grads[kind][None]
        outputs.append(full)
        outputs.extend(
            adam_step(
                weights[kind], firsts[kind], seconds[kind], full, RATES[kind], DECAYS[kind]
            )
        )
    return tuple(outputs)


def solution(mesh):
    by_axis = jax.sharding.Mesh(mesh.devices.reshape(4, 2, 2, 4, 2), AXES)
    along_ctx, along_fsdp = ("x", "zl"), ("zh", "y", "core")
    by_token = P(along_fsdp, along_ctx, None)
    by_row = P(None, AXES, None)
    return jax.shard_map(
        body,
        mesh=by_axis,
        in_specs=(by_token, by_token, P(along_fsdp, None), P(along_fsdp, along_ctx))
        + (by_row,) * 24,
        out_specs=(by_token, by_token) + (by_row,) * 32,
        check_vma=False,
    )
```

time: 3950 us -> 512 us (0.13)
  waiting for transfers between devices: 3150 us -> 160 us
  matrix products: 306 us -> 1.3 us
  blocking collectives: 236 us -> 0 us
  other arithmetic: 162 us -> 22.3 us
  Pallas kernels: 0 us -> 136 us
  starting transfers between devices: 0.71 us -> 124 us
    unnamed x16 -> x2, waiting for transfers between devices: 1250 us -> 0.03 us
    all_gather x7 -> x1, waiting for transfers between devices: 1230 us -> 0.01 us  [body(): mlp_full = lax.all_gather(mlp_rows, SHARE, axis=0, tiled=True)]
    reduce_scatter x1, waiting for transfers between devices: 665 us -> 0.01 us  [body(): lax.psum_scatter(terms.reshape(-1, D), SHARE, scatter_dimension=0, tiled=...]
    dot_general x25 -> x1, matrix products: 306 us -> 1.3 us  [dot(): lax.dot_general(left, right, dims, preferred_element_type=f32).astype(kind)]
    all_gather x3 -> x0, blocking collectives: 236 us -> none  [the longest x1 182 us: attention_weights(): lax.all_gather(pieces[4], ('ctx', 'fsdp'), axis=0, tiled=True)]
    ppermute x0 -> x88, waiting for transfers between devices: none -> 160 us  [the longest x4 30.5 us: scatter_parts(): got_left = lax.ppermute(left, name, to_left)]
    pallas_call x0 -> x22, Pallas kernels: none -> 136 us  [the longest x19 120 us: call(): pl.pallas_call(kernel, out_shape=[jax.ShapeDtypeStruct(shape, kind) for s...]
    ppermute x0 -> x88, starting transfers between devices: none -> 124 us  [the longest x4 15.7 us: ring_sum_small(): lax.ppermute(to_left, name, left)]
  transfers between devices with their start and end apart: 12 -> 90, of which waited for: 10 -> 35; matrix products, arithmetic and copies ran while one was open for 9% -> 7% of each run, Pallas kernels for 0% -> 18%
where the time goes in v1:
time: 512 us; the launch traced here: 503 us
  waiting for transfers between devices  160 us (31%)
  Pallas kernels  136 us (27%)
  starting transfers between devices  124 us (24%)
  local copies, waits for them, and re-layouts  43.6 us (9%)
  other arithmetic  22.3 us (4%)
  between operations  15.9 us (3%)
    pallas_call x19, Pallas kernels, call(): pl.pallas_call(kernel, out_shape=[jax.ShapeDtypeStruct(shape, kind) for s...  120 us
    ppermute x4, waiting for transfers between devices, scatter_parts(): got_left = lax.ppermute(left, name, to_left)  30.5 us
    unnamed x230, local copies, waits for them, and re-layouts  27.1 us
    ppermute x4, waiting for transfers between devices, ring_small(): lax.ppermute(block, name, across(ring))  25.1 us
    ppermute x4, waiting for transfers between devices, ring_halves(): first = lax.ppermute(from_left[:half], name, right)  19.3 us
    ppermute x4, waiting for transfers between devices, ring_small(): lax.ppermute(block, name, right)  18 us
    pallas_call x3, Pallas kernels, mlp_grad(): pl.pallas_call(mlp_grad_kernel, grid=(D // width,), out_shape=jax.ShapeDt...  16.1 us
    ppermute x4, starting transfers between devices, ring_sum_small(): lax.ppermute(to_left, name, left)  15.7 us
  transfers between devices with their start and end apart: 90, of which 35 were waited for; matrix products, arithmetic and copies ran while one was open for 7% of the time, Pallas kernels for 18%

profile of v1, /device:TPU:0, one launch (start us, length us, event | category | flops | bytes accessed | tf_op | source)
XLA Modules:
  0.0 502.6 jit_solution(16188173671554084507)
XLA Ops:
  22.0 8.6 %collective-permute-done.4.refs_1_ = bf16[16,768]{1,0:T(8,128)(2,1)S(1)} collective-permute-done((bf16[16,768]{1,0:T(8,128)(2,1)S(1)}, bf16[16,768]{1,0:T(8,128)(2,1)S(1)}, u32[]{:S(2)}, u32[]{:S(2)}) %collective-permute-start.4) | collective-permute-done | bytes 24608 | tf_op jit(solution)/shard_map/ppermute | solution.py:651
  39.5 2.3 collective-permute-done.7.refs_1_
  46.3 3.9 collective-permute-start.12
  51.5 2.2 collective-permute-start.11
  54.5 13.8 %collective-permute-done.12.refs_8_ = bf16[256,768]{1,0:T(8,128)(2,1)S(1)} collective-permute-done((bf16[256,768]{1,0:T(8,128)(2,1)}, bf16[256,768]{1,0:T(8,128)(2,1)S(1)}, u32[]{:S(2)}, u32[]{:S(2)}) %collective-permute-start.12) | collective-permute-done | bytes 393248 | tf_op jit(solution)/shard_map/ppermute | solution.py:94
  69.0 6.6 %collective-permute-done.18.refs_1_ = bf16[16,2048]{1,0:T(8,128)(2,1)S(1)} collective-permute-done((bf16[16,2048]{1,0:T(8,128)(2,1)S(1)}, bf16[16,2048]{1,0:T(8,128)(2,1)S(1)}, u32[]{:S(2)}, u32[]{:S(2)}) %collective-permute-start.18) | collective-permute-done | bytes 65568 | tf_op jit(solution)/shard_map/ppermute | solution.py:92
  75.8 4.8 collective-permute-done.19.refs_2_
  81.6 5.9 %collective-permute-done.20.refs_3_ = bf16[16,2048]{1,0:T(8,128)(2,1)S(1)} collective-permute-done((bf16[16,2048]{1,0:T(8,128)(2,1)S(1)}, bf16[16,2048]{1,0:T(8,128)(2,1)S(1)}, u32[]{:S(2)}, u32[]{:S(2)}) %collective-permute-start.20) | collective-permute-done | bytes 65568 | tf_op jit(solution)/shard_map/ppermute | solution.py:94
  87.5 3.4 collective-permute-start.3
  95.3 3.3 collective-permute-start.22
  98.6 9.2 %collective-permute-done.21.refs_6_ = bf16[64,2048]{1,0:T(8,128)(2,1)} collective-permute-done((bf16[64,2048]{1,0:T(8,128)(2,1)}, bf16[64,2048]{1,0:T(8,128)(2,1)}, u32[]{:S(2)}, u32[]{:S(2)}) %collective-permute-start.21) | collective-permute-done | bytes 262176 | tf_op jit(solution)/shard_map/ppermute | solution.py:92
  107.8 2.4 collective-permute-start.23
  112.8 3.3 collective-permute-done.23.refs_8_
  117.7 8.1 %shard_map.534 = (bf16[512,512]{1,0:T(8,128)(2,1)}, bf16[512,128]{1,0:T(8,128)(2,1)}, bf16[512,2048]{1,0:T(8,128)(2,1)}, bf16[2048,640]{1,0:T(8,128)(2,1)}, bf16...) custom-call(s32[14]{0:T(128)} %stack.99.spots, bf16[128,2176]{1,0:T(8,128)(2,1)} %shard_map.531.refs_0_, ...), custom_call_target="tpu_custom_call" | custom-call | flops 1342177280 | bytes 12582912 | tf_op jit(solution)/shard_map/pallas_call | solution.py:150
  127.9 4.0 collective-permute-done.17.refs_2_.other_ref
  132.6 12.3 %shard_map.536 = (bf16[512,512]{1,0:T(8,128)(2,1)}, f32[512,128]{1,0:T(8,128)}, bf16[512,2048]{1,0:T(8,128)(2,1)}, bf16[128,2048]{1,0:T(8,128)(2,1)}, bf16[128,2...) custom-call(s32[14]{0:T(128)} %stack.99.spots, ...), custom_call_target="tpu_custom_call" | custom-call | flops 5368709120 | bytes 12582912 | tf_op jit(solution)/shard_map/pallas_call | solution.py:150
  147.7 2.5 collective-permute-start.42
  150.2 9.8 %collective-permute-done.28.left = bf16[128,2048]{1,0:T(8,128)(2,1)S(1)} collective-permute-done((bf16[128,2048]{1,0:T(8,128)(2,1)}, bf16[128,2048]{1,0:T(8,128)(2,1)S(1)}, u32[]{:S(2)}, u32[]{:S(2)}) %collective-permute-start.28) | collective-permute-done | bytes 524320 | tf_op jit(solution)/shard_map/ppermute | solution.py:365
  161.2 3.2 collective-permute-start.30
  165.6 12.7 %collective-permute-start.31 = (bf16[64,2048]{1,0:T(8,128)(2,1)S(1)}, bf16[64,2048]{1,0:T(8,128)(2,1)S(1)}, u32[]{:S(2)}, u32[]{:S(2)}) collective-permute-start(bf16[64,2048]{1,0:T(8,128)(2,1)S(1)} %add_convert_fusion.16), channel_id=1, source_target_pairs={{0,32},{32,64},{64,96},{96,0},{1,33},{33,65},{65,97},{97,1},{2,34}... | collective-permute-start | bytes 786440 | tf_op jit(solution)/shard_map/ppermute | solution.py:369
  179.1 6.7 %collective-permute-done.31.high = bf16[64,2048]{1,0:T(8,128)(2,1)S(1)} collective-permute-done((bf16[64,2048]{1,0:T(8,128)(2,1)S(1)}, bf16[64,2048]{1,0:T(8,128)(2,1)S(1)}, u32[]{:S(2)}, u32[]{:S(2)}) %collective-permute-start.31) | collective-permute-done | bytes 262176 | tf_op jit(solution)/shard_map/ppermute | solution.py:369
  186.6 3.2 shard_map.537
  189.8 3.3 collective-permute-start.33
  193.1 3.3 collective-permute-start.44
  196.4 10.1 %collective-permute-done.43.refs_13_ = bf16[64,2048]{1,0:T(8,128)(2,1)S(1)} collective-permute-done((bf16[64,2048]{1,0:T(8,128)(2,1)S(1)}, bf16[64,2048]{1,0:T(8,128)(2,1)S(1)}, u32[]{:S(2)}, u32[]{:S(2)}) %collective-permute-start.43) | collective-permute-done | bytes 262176 | tf_op jit(solution)/shard_map/ppermute | solution.py:83
  209.9 2.9 collective-permute-start.35
  213.4 5.7 %collective-permute-done.34.refs_3_ = bf16[64,2048]{1,0:T(8,128)(2,1)S(1)} collective-permute-done((bf16[64,2048]{1,0:T(8,128)(2,1)S(1)}, bf16[64,2048]{1,0:T(8,128)(2,1)S(1)}, u32[]{:S(2)}, u32[]{:S(2)}) %collective-permute-start.34) | collective-permute-done | bytes 262176 | tf_op jit(solution)/shard_map/ppermute | solution.py:83
  222.6 29.5 %shard_map.538 = (bf16[128,2048]{1,0:T(8,128)(2,1)}, bf16[128,2048]{1,0:T(8,128)(2,1)}, bf16[128,2048]{1,0:T(8,128)(2,1)}, bf16[64,2048]{1,0:T(8,128)(2,1)}, bf1...) custom-call(bf16[128,2048]{1,0:T(8,128)(2,1)} %get-tuple-element.101, ...), custom_call_target="tpu_custom_call" | custom-call | flops 16106127360 | bytes 31457280 | tf_op jit(solution)/shard_map/pallas_call | solution.py:150
  252.1 2.2 copy-done
  255.7 5.3 %shard_map.550.refs_0_ = bf16[16,144,2048]{2,1,0:T(8,128)(2,1)} custom-call(bf16[1024,768]{1,0:T(8,128)(2,1)S(1)} %copy-done.4, bf16[1024,2048]{1,0:T(8,128)(2,1)S(1)} %copy-done), custom_call_target="tpu_custom_call" | custom-call | flops 3221225472 | bytes 8388608 | tf_op jit(solution)/shard_map/pallas_call | solution.py:485
  261.0 5.4 %shard_map.551.refs_0_ = bf16[16,144,2048]{2,1,0:T(8,128)(2,1)} custom-call(bf16[1024,768]{1,0:T(8,128)(2,1)S(1)} %copy-done.3, bf16[1024,2048]{1,0:T(8,128)(2,1)S(1)} %copy-done, bf16[16,144,2048]{2,1,0:T(8,128)(2,1)} %shard_map.550.refs_0_), custom_call_target="tpu_custom_call", output_to_operand_aliasing={{}: (2, {})} | custom-call | flops 3221225472 | bytes 8388608 | tf_op jit(solution)/shard_map/pallas_call | solution.py:485
  266.4 5.4 %shard_map.552 = bf16[16,144,2048]{2,1,0:T(8,128)(2,1)} custom-call(bf16[1024,768]{1,0:T(8,128)(2,1)S(1)} %copy-done.2, bf16[1024,2048]{1,0:T(8,128)(2,1)S(1)} %copy-done.1, bf16[16,144,2048]{2,1,0:T(8,128)(2,1)} %shard_map.551.refs_0_), custom_call_target="tpu_custom_call", output_to_operand_aliasing={{}: (2, {})} | custom-call | flops 3221225472 | bytes 8388608 | tf_op jit(solution)/shard_map/pallas_call | solution.py:485
  275.1 2.7 collective-permute-start.52
  277.8 11.5 %collective-permute-done.52.left = bf16[128,2048]{1,0:T(8,128)(2,1)S(1)} collective-permute-done((bf16[128,2048]{1,0:T(8,128)(2,1)S(1)}, bf16[128,2048]{1,0:T(8,128)(2,1)S(1)}, u32[]{:S(2)}, u32[]{:S(2)}) %collective-permute-start.52) | collective-permute-done | bytes 524320 | tf_op jit(solution)/shard_map/ppermute | solution.py:365
  289.3 3.4 collective-permute-done.53.right
  296.0 4.3 collective-permute-done.54.low
  302.6 4.0 shard_map.539
  306.8 3.0 collective-permute-start.57
  309.8 10.3 %collective-permute-done.56.refs_1_ = bf16[128,2048]{1,0:T(8,128)(2,1)S(1)} collective-permute-done((bf16[128,2048]{1,0:T(8,128)(2,1)}, bf16[128,2048]{1,0:T(8,128)(2,1)S(1)}, u32[]{:S(2)}, u32[]{:S(2)}) %collective-permute-start.56) | collective-permute-done | bytes 524320 | tf_op jit(solution)/shard_map/ppermute | solution.py:81
  320.7 3.3 collective-permute-start.59
  324.7 3.5 collective-permute-done.58.refs_3_
  329.0 5.3 %shard_map.540 = (bf16[512,2048]{1,0:T(8,128)(2,1)}, bf16[512,512]{1,0:T(8,128)(2,1)}) custom-call(bf16[128,2048]{1,0:T(8,128)(2,1)} %get-tuple-element.111.refs_0_, bf16[128,2048]{1,0:T(8,128)(2,1)} %copy-done.21, bf16[128,2048]{1,0:T(8,128)(2,1)} %copy-done.22, bf16[64,2048]{1,0:T(8,128)(2,1)} %copy-done.47, bf16[64,2048]{1,0:T(8,128)(2,1)} %copy-done.48, ...), custom_call_target="tpu_custom_call" | custom-call | flops 1073741824 | bytes 6291456 | tf_op jit(solution)/shard_map/pallas_call | solution.py:150
  334.3 6.0 %shard_map.543 = (bf16[512,128]{1,0:T(8,128)(2,1)}, f32[1024,128]{1,0:T(8,128)}) custom-call(bf16[512,512]{1,0:T(8,128)(2,1)} %get-tuple-element.92.refs_0_.query_ref, bf16[512,128]{1,0:T(8,128)(2,1)} %get-tuple-element.93.refs_1_.own_ref, bf16[512,128]{1,0:T(8,128)(2,1)} %copy-done.103, s32[512,1]{1,0:T(8,128)} %broadcast_in_dim.57.refs_3_.row_ref, ...), custom_call_target="tpu_custom_call" | custom-call | flops 2684354560 | bytes 4194304 | tf_op jit(solution)/shard_map/pallas_call | solution.py:150
  340.3 6.6 %shard_map.544 = (bf16[512,128]{1,0:T(8,128)(2,1)}, f32[1024,128]{1,0:T(8,128)}) custom-call(bf16[512,512]{1,0:T(8,128)(2,1)} %get-tuple-element.92.refs_0_.query_ref, bf16[512,128]{1,0:T(8,128)(2,1)} %get-tuple-element.93.refs_1_.own_ref, bf16[512,128]{1,0:T(8,128)(2,1)} %copy-done.103, s32[512,1]{1,0:T(8,128)} %broadcast_in_dim.57.refs_3_.row_ref, ...), custom_call_target="tpu_custom_call" | custom-call | flops 2684354560 | bytes 4194304 | tf_op jit(solution)/shard_map/pallas_call | solution.py:150
  346.9 6.2 %shard_map.545 = (bf16[512,128]{1,0:T(8,128)(2,1)}, f32[1024,128]{1,0:T(8,128)}) custom-call(bf16[512,512]{1,0:T(8,128)(2,1)} %get-tuple-element.92.refs_0_.query_ref, bf16[512,128]{1,0:T(8,128)(2,1)} %get-tuple-element.93.refs_1_.own_ref, bf16[512,128]{1,0:T(8,128)(2,1)} %copy-done.103, s32[512,1]{1,0:T(8,128)} %broadcast_in_dim.57.refs_3_.row_ref, ...), custom_call_target="tpu_custom_call" | custom-call | flops 2684354560 | bytes 4194304 | tf_op jit(solution)/shard_map/pallas_call | solution.py:150
  353.1 6.4 %shard_map.546 = (bf16[512,128]{1,0:T(8,128)(2,1)}, f32[1024,128]{1,0:T(8,128)}) custom-call(bf16[512,512]{1,0:T(8,128)(2,1)} %get-tuple-element.92.refs_0_.query_ref, bf16[512,128]{1,0:T(8,128)(2,1)} %get-tuple-element.93.refs_1_.own_ref, bf16[512,128]{1,0:T(8,128)(2,1)} %copy-done.103, s32[512,1]{1,0:T(8,128)} %broadcast_in_dim.57.refs_3_.row_ref, ...), custom_call_target="tpu_custom_call" | custom-call | flops 2684354560 | bytes 4194304 | tf_op jit(solution)/shard_map/pallas_call | solution.py:150
  360.9 8.1 %shard_map.541 = (bf16[128,2048]{1,0:T(8,128)(2,1)}, bf16[128,2048]{1,0:T(8,128)(2,1)}, bf16[128,2048]{1,0:T(8,128)(2,1)}, bf16[64,2048]{1,0:T(8,128)(2,1)}, bf1...) custom-call(bf16[1024,768]{1,0:T(8,128)(2,1)} %get-tuple-element.114.hidden_ref.left_ref, ...), custom_call_target="tpu_custom_call" | custom-call | flops 3221225472 | bytes 8388608 | tf_op jit(solution)/shard_map/pallas_call | solution.py:150
  370.3 5.4 %shard_map.547 = (bf16[512,640]{1,0:T(8,128)(2,1)}, bf16[128,2048]{1,0:T(8,128)(2,1)}, bf16[128,2048]{1,0:T(8,128)(2,1)}, bf16[128,2048]{1,0:T(8,128)(2,1)}, bf1...) custom-call(bf16[512,128]{1,0:T(8,128)(2,1)} %get-tuple-element.126.query0, bf16[512,128]{1,0:T(8,128)(2,1)} %get-tuple-element.128.query1, ...), custom_call_target="tpu_custom_call" | custom-call | flops 1342177280 | bytes 8388608 | tf_op jit(solution)/shard_map/pallas_call | solution.py:150
  375.7 3.6 collective-permute-start.67
  381.9 9.2 %collective-permute-done.67.left = bf16[128,2048]{1,0:T(8,128)(2,1)S(1)} collective-permute-done((bf16[128,2048]{1,0:T(8,128)(2,1)}, bf16[128,2048]{1,0:T(8,128)(2,1)S(1)}, u32[]{:S(2)}, u32[]{:S(2)}) %collective-permute-start.67) | collective-permute-done | bytes 524320 | tf_op jit(solution)/shard_map/ppermute | solution.py:365
  391.1 3.7 collective-permute-start.69
  397.1 5.4 %shard_map.549 = bf16[2048,768]{1,0:T(8,128)(2,1)} custom-call(bf16[512,2048]{1,0:T(8,128)(2,1)} %get-tuple-element.140.normed_ref, bf16[512,640]{1,0:T(8,128)(2,1)} %get-tuple-element.141.proj_ref, bf16[2048,128]{1,0:T(8,128)(2,1)} %broadcast_in_dim.51.gain_ref), custom_call_target="tpu_custom_call" | custom-call | flops 1342177280 | bytes 6291456 | tf_op jit(solution)/shard_map/pallas_call | solution.py:150
  405.0 3.7 shard_map.548
  409.1 3.2 collective-permute-start.62
  418.1 3.2 collective-permute-start.82
  422.0 2.9 collective-permute-done.84
  426.8 3.6 collective-permute-done.83
  430.9 7.9 %collective-permute-start.72 = (bf16[4,4,16,768]{3,2,1,0:T(8,128)(2,1)S(1)}, bf16[4,4,16,768]{3,2,1,0:T(8,128)(2,1)S(1)}, u32[]{:S(2)}, u32[]{:S(2)}) collective-permute-start(bf16[4,4,16,768]{3,2,1,0:T(8,128)(2,1)S(1)} %get-tuple-element.244), channel_id=1, source_target_pairs={{0,24},{16,0},{8,16},{24,8},{1,25},{17,1},{9,17},{25,9},{2,26},{18... | collective-permute-start | bytes 1179656 | tf_op jit(solution)/shard_map/ppermute | solution.py:102
  440.3 6.3 %collective-permute-done.73 = bf16[4,4,16,768]{3,2,1,0:T(8,128)(2,1)S(1)} collective-permute-done((bf16[4,4,16,768]{3,2,1,0:T(8,128)(2,1)S(1)}, bf16[4,4,16,768]{3,2,1,0:T(8,128)(2,1)S(1)}, u32[]{:S(2)}, u32[]{:S(2)}) %collective-permute-start.73) | collective-permute-done | bytes 393248 | tf_op jit(solution)/shard_map/ppermute | solution.py:103
  446.9 2.5 collective-permute-start.77
  454.2 3.0 collective-permute-start.85
  457.2 2.9 collective-permute-start.64
  460.3 3.3 collective-permute-start.79
  469.0 2.8 shard_map.542
  (468 shorter events, 124.2 us)
Async XLA Ops:
  7.2 215.3 %all-gather.2.cloned.1.call-start = ((), (), s32[]{:S(2)}) async-start(), calls=%async_computation.1 | async-start | bytes 10027008 | tf_op jit(solution)/shard_map/all_gather | solution.py:634
  10.9 467.7 %reduce-scatter.2.cloned.1.call-start = ((), (), s32[]{:S(2)}) async-start(), calls=%async_computation.2 | async-start | bytes 10027008 | tf_op jit(solution)/shard_map/reduce_scatter | solution.py:739
  14.3 39.4 %collective-permute-start = (bf16[128,2176]{1,0:T(8,128)(2,1)}, bf16[128,2176]{1,0:T(8,128)(2,1)S(1)}, u32[]{:S(2)}, u32[]{:S(2)}) collective-permute-start(bf16[128,2176]{1,0:T(8,128)(2,1)} %shard_map.531.refs_0_), channel_id=1, source_target_pairs={{0,32},{32,64},{64,96},{96,0},{1,33},{33,65},{65,97},{97,1},{2,34}... | collective-permute-start | bytes 1671176 | tf_op jit(solution)/shard_map/ppermute | solution.py:81
  17.2 13.4 %collective-permute-start.4 = (bf16[16,768]{1,0:T(8,128)(2,1)S(1)}, bf16[16,768]{1,0:T(8,128)(2,1)S(1)}, u32[]{:S(2)}, u32[]{:S(2)}) collective-permute-start(bf16[16,768]{1,0:T(8,128)(2,1)S(1)} %get-tuple-element.281), channel_id=1, source_target_pairs={{0,32},{32,64},{64,96},{96,0},{1,33},{33,65},{65,97},{97,1},{2,34}... | collective-permute-start | bytes 73736 | tf_op jit(solution)/shard_map/ppermute | solution.py:651
  18.7 11.9 %collective-permute-start.5 = (bf16[16,768]{1,0:T(8,128)(2,1)S(1)}, bf16[16,768]{1,0:T(8,128)(2,1)S(1)}, u32[]{:S(2)}, u32[]{:S(2)}) collective-permute-start(bf16[16,768]{1,0:T(8,128)(2,1)S(1)} %get-tuple-element.280), channel_id=1, source_target_pairs={{0,96},{32,0},{64,32},{96,64},{1,97},{33,1},{65,33},{97,65},{2,98}... | collective-permute-start | bytes 73736 | tf_op jit(solution)/shard_map/ppermute | solution.py:652
  20.5 11.8 %collective-permute-start.6 = (bf16[16,768]{1,0:T(8,128)(2,1)S(1)}, bf16[16,768]{1,0:T(8,128)(2,1)S(1)}, u32[]{:S(2)}, u32[]{:S(2)}) collective-permute-start(bf16[16,768]{1,0:T(8,128)(2,1)S(1)} %get-tuple-element.279), channel_id=1, source_target_pairs={{0,64},{32,96},{64,0},{96,32},{1,65},{33,97},{65,1},{97,33},{2,66}... | collective-permute-start | bytes 73736 | tf_op jit(solution)/shard_map/ppermute | solution.py:653
  46.3 22.1 %collective-permute-start.12 = (bf16[256,768]{1,0:T(8,128)(2,1)}, bf16[256,768]{1,0:T(8,128)(2,1)S(1)}, u32[]{:S(2)}, u32[]{:S(2)}) collective-permute-start(bf16[256,768]{1,0:T(8,128)(2,1)} %shard_map.533.refs_5_), channel_id=1, source_target_pairs={{0,8},{16,24},{8,0},{24,16},{1,9},{17,25},{9,1},{25,17},{2,10},{18... | collective-permute-start | bytes 1179656 | tf_op jit(solution)/shard_map/ppermute | solution.py:94
  50.2 18.7 %collective-permute-start.1 = (bf16[128,2176]{1,0:T(8,128)(2,1)S(1)}, bf16[128,2176]{1,0:T(8,128)(2,1)S(1)}, u32[]{:S(2)}, u32[]{:S(2)}) collective-permute-start(bf16[128,2176]{1,0:T(8,128)(2,1)S(1)} %copy-done.7), channel_id=1, source_target_pairs={{0,96},{32,0},{64,32},{96,64},{1,97},{33,1},{65,33},{97,65},{2,98}... | collective-permute-start | bytes 1671176 | tf_op jit(solution)/shard_map/ppermute | solution.py:82
  50.5 42.1 %collective-permute-start.10 = (bf16[256,768]{1,0:T(8,128)(2,1)}, bf16[256,768]{1,0:T(8,128)(2,1)S(1)}, u32[]{:S(2)}, u32[]{:S(2)}) collective-permute-start(bf16[256,768]{1,0:T(8,128)(2,1)} %shard_map.533.refs_5_), channel_id=1, source_target_pairs={{0,16},{16,8},{8,24},{24,0},{1,17},{17,9},{9,25},{25,1},{2,18},{18... | collective-permute-start | bytes 1179656 | tf_op jit(solution)/shard_map/ppermute | solution.py:92
  51.5 43.0 %collective-permute-start.11 = (bf16[256,768]{1,0:T(8,128)(2,1)}, bf16[256,768]{1,0:T(8,128)(2,1)S(1)}, u32[]{:S(2)}, u32[]{:S(2)}) collective-permute-start(bf16[256,768]{1,0:T(8,128)(2,1)} %shard_map.533.refs_5_), channel_id=1, source_target_pairs={{0,24},{16,0},{8,16},{24,8},{1,25},{17,1},{9,17},{25,9},{2,26},{18... | collective-permute-start | bytes 1179656 | tf_op jit(solution)/shard_map/ppermute | solution.py:93
  53.7 40.9 %collective-permute-start.13 = (bf16[256,768]{1,0:T(8,128)(2,1)}, bf16[256,768]{1,0:T(8,128)(2,1)}, u32[]{:S(2)}, u32[]{:S(2)}) collective-permute-start(bf16[256,768]{1,0:T(8,128)(2,1)} %shard_map.533.refs_5_), channel_id=1, source_target_pairs={{0,1},{1,0},{2,3},{3,2},{4,5},{5,4},{6,7},{7,6},{8,9},{9,8},{10,11... | collective-permute-start | bytes 1179656 | tf_op jit(solution)/shard_map/ppermute | solution.py:657
  68.4 26.8 %collective-permute-start.2 = (bf16[64,2176]{1,0:T(8,128)(2,1)}, bf16[64,2176]{1,0:T(8,128)(2,1)}, u32[]{:S(2)}, u32[]{:S(2)}) collective-permute-start(bf16[64,2176]{1,0:T(8,128)(2,1)} %slice.162), channel_id=1, source_target_pairs={{0,32},{32,64},{64,96},{96,0},{1,33},{33,65},{65,97},{97,1},{2,34}... | collective-permute-start | bytes 835592 | tf_op jit(solution)/shard_map/ppermute | solution.py:83
  92.6 15.2 %collective-permute-start.21 = (bf16[64,2048]{1,0:T(8,128)(2,1)}, bf16[64,2048]{1,0:T(8,128)(2,1)}, u32[]{:S(2)}, u32[]{:S(2)}) collective-permute-start(bf16[64,2048]{1,0:T(8,128)(2,1)} %shard_map.535.refs_5_), channel_id=1, source_target_pairs={{0,16},{16,8},{8,24},{24,0},{1,17},{17,9},{9,25},{25,1},{2,18},{18... | collective-permute-start | bytes 786440 | tf_op jit(solution)/shard_map/ppermute | solution.py:92
  94.5 22.3 %collective-permute-start.16 = (bf16[256,768]{1,0:T(8,128)(2,1)S(1)}, bf16[256,768]{1,0:T(8,128)(2,1)S(1)}, u32[]{:S(2)}, u32[]{:S(2)}) collective-permute-start(bf16[256,768]{1,0:T(8,128)(2,1)S(1)} %collective-permute-done.12.refs_8_), channel_id=1, source_target_pairs={{0,1},{1,0},{2,3},{3,2},{4,5},{5,4},{6,7},{7,6},{8,9},{9,8},{10,11... | collective-permute-start | bytes 1179656 | tf_op jit(solution)/shard_map/ppermute | solution.py:657
  94.6 21.4 %collective-permute-start.14 = (bf16[256,768]{1,0:T(8,128)(2,1)S(1)}, bf16[256,768]{1,0:T(8,128)(2,1)}, u32[]{:S(2)}, u32[]{:S(2)}) collective-permute-start(bf16[256,768]{1,0:T(8,128)(2,1)S(1)} %collective-permute-done.10.refs_6_), channel_id=1, source_target_pairs={{0,1},{1,0},{2,3},{3,2},{4,5},{5,4},{6,7},{7,6},{8,9},{9,8},{10,11... | collective-permute-start | bytes 1179656 | tf_op jit(solution)/shard_map/ppermute | solution.py:657
  95.1 21.4 %collective-permute-start.15 = (bf16[256,768]{1,0:T(8,128)(2,1)S(1)}, bf16[256,768]{1,0:T(8,128)(2,1)}, u32[]{:S(2)}, u32[]{:S(2)}) collective-permute-start(bf16[256,768]{1,0:T(8,128)(2,1)S(1)} %collective-permute-done.11.refs_7_), channel_id=1, source_target_pairs={{0,1},{1,0},{2,3},{3,2},{4,5},{5,4},{6,7},{7,6},{8,9},{9,8},{10,11... | collective-permute-start | bytes 1179656 | tf_op jit(solution)/shard_map/ppermute | solution.py:657
  95.3 17.4 %collective-permute-start.22 = (bf16[64,2048]{1,0:T(8,128)(2,1)}, bf16[64,2048]{1,0:T(8,128)(2,1)}, u32[]{:S(2)}, u32[]{:S(2)}) collective-permute-start(bf16[64,2048]{1,0:T(8,128)(2,1)} %shard_map.535.refs_5_), channel_id=1, source_target_pairs={{0,24},{16,0},{8,16},{24,8},{1,25},{17,1},{9,17},{25,9},{2,26},{18... | collective-permute-start | bytes 786440 | tf_op jit(solution)/shard_map/ppermute | solution.py:93
  112.7 15.2 %collective-permute-start.24 = (bf16[64,2048]{1,0:T(8,128)(2,1)}, bf16[64,2048]{1,0:T(8,128)(2,1)}, u32[]{:S(2)}, u32[]{:S(2)}) collective-permute-start(bf16[64,2048]{1,0:T(8,128)(2,1)} %shard_map.535.refs_5_), channel_id=1, source_target_pairs={{0,1},{1,0},{2,3},{3,2},{4,5},{5,4},{6,7},{7,6},{8,9},{9,8},{10,11... | collective-permute-start | bytes 786440 | tf_op jit(solution)/shard_map/ppermute | solution.py:694
  116.0 15.9 %collective-permute-start.25 = (bf16[64,2048]{1,0:T(8,128)(2,1)}, bf16[64,2048]{1,0:T(8,128)(2,1)}, u32[]{:S(2)}, u32[]{:S(2)}) collective-permute-start(bf16[64,2048]{1,0:T(8,128)(2,1)} %collective-permute-done.21.refs_6_), channel_id=1, source_target_pairs={{0,1},{1,0},{2,3},{3,2},{4,5},{5,4},{6,7},{7,6},{8,9},{9,8},{10,11... | collective-permute-start | bytes 786440 | tf_op jit(solution)/shard_map/ppermute | solution.py:694
  116.0 15.9 %collective-permute-start.26 = (bf16[64,2048]{1,0:T(8,128)(2,1)}, bf16[64,2048]{1,0:T(8,128)(2,1)}, u32[]{:S(2)}, u32[]{:S(2)}) collective-permute-start(bf16[64,2048]{1,0:T(8,128)(2,1)} %collective-permute-done.22.refs_7_), channel_id=1, source_target_pairs={{0,1},{1,0},{2,3},{3,2},{4,5},{5,4},{6,7},{7,6},{8,9},{9,8},{10,11... | collective-permute-start | bytes 786440 | tf_op jit(solution)/shard_map/ppermute | solution.py:694
  116.5 15.4 %collective-permute-start.27 = (bf16[64,2048]{1,0:T(8,128)(2,1)}, bf16[64,2048]{1,0:T(8,128)(2,1)}, u32[]{:S(2)}, u32[]{:S(2)}) collective-permute-start(bf16[64,2048]{1,0:T(8,128)(2,1)} %collective-permute-done.23.refs_8_), channel_id=1, source_target_pairs={{0,1},{1,0},{2,3},{3,2},{4,5},{5,4},{6,7},{7,6},{8,9},{9,8},{10,11... | collective-permute-start | bytes 786440 | tf_op jit(solution)/shard_map/ppermute | solution.py:694
  144.9 15.1 %collective-permute-start.28 = (bf16[128,2048]{1,0:T(8,128)(2,1)}, bf16[128,2048]{1,0:T(8,128)(2,1)S(1)}, u32[]{:S(2)}, u32[]{:S(2)}) collective-permute-start(bf16[128,2048]{1,0:T(8,128)(2,1)} %get-tuple-element.96), channel_id=1, source_target_pairs={{0,96},{32,0},{64,32},{96,64},{1,97},{33,1},{65,33},{97,65},{2,98}... | collective-permute-start | bytes 1572872 | tf_op jit(solution)/shard_map/ppermute | solution.py:365
  146.9 17.5 %collective-permute-start.29 = (bf16[128,2048]{1,0:T(8,128)(2,1)}, bf16[128,2048]{1,0:T(8,128)(2,1)S(1)}, u32[]{:S(2)}, u32[]{:S(2)}) collective-permute-start(bf16[128,2048]{1,0:T(8,128)(2,1)} %get-tuple-element.97), channel_id=1, source_target_pairs={{0,32},{32,64},{64,96},{96,0},{1,33},{33,65},{65,97},{97,1},{2,34}... | collective-permute-start | bytes 1572872 | tf_op jit(solution)/shard_map/ppermute | solution.py:366
  147.0 42.8 %collective-permute-start.41 = (bf16[128,2048]{1,0:T(8,128)(2,1)S(1)}, bf16[128,2048]{1,0:T(8,128)(2,1)S(1)}, u32[]{:S(2)}, u32[]{:S(2)}) collective-permute-start(bf16[128,2048]{1,0:T(8,128)(2,1)S(1)} %bitcast.164), channel_id=1, source_target_pairs={{0,32},{32,64},{64,96},{96,0},{1,33},{33,65},{65,97},{97,1},{2,34}... | collective-permute-start | bytes 1572872 | tf_op jit(solution)/shard_map/ppermute | solution.py:81
  147.7 45.4 %collective-permute-start.42 = (bf16[128,2048]{1,0:T(8,128)(2,1)S(1)}, bf16[128,2048]{1,0:T(8,128)(2,1)S(1)}, u32[]{:S(2)}, u32[]{:S(2)}) collective-permute-start(bf16[128,2048]{1,0:T(8,128)(2,1)S(1)} %bitcast.165), channel_id=1, source_target_pairs={{0,96},{32,0},{64,32},{96,64},{1,97},{33,1},{65,33},{97,65},{2,98}... | collective-permute-start | bytes 1572872 | tf_op jit(solution)/shard_map/ppermute | solution.py:82
  161.2 17.9 %collective-permute-start.30 = (bf16[64,2048]{1,0:T(8,128)(2,1)S(1)}, bf16[64,2048]{1,0:T(8,128)(2,1)S(1)}, u32[]{:S(2)}, u32[]{:S(2)}) collective-permute-start(bf16[64,2048]{1,0:T(8,128)(2,1)S(1)} %add_convert_fusion.17), channel_id=1, source_target_pairs={{0,96},{32,0},{64,32},{96,64},{1,97},{33,1},{65,33},{97,65},{2,98}... | collective-permute-start | bytes 786440 | tf_op jit(solution)/shard_map/ppermute | solution.py:369
  165.6 20.3 %collective-permute-start.31 = (bf16[64,2048]{1,0:T(8,128)(2,1)S(1)}, bf16[64,2048]{1,0:T(8,128)(2,1)S(1)}, u32[]{:S(2)}, u32[]{:S(2)}) collective-permute-start(bf16[64,2048]{1,0:T(8,128)(2,1)S(1)} %add_convert_fusion.16), channel_id=1, source_target_pairs={{0,32},{32,64},{64,96},{96,0},{1,33},{33,65},{65,97},{97,1},{2,34}... | collective-permute-start | bytes 786440 | tf_op jit(solution)/shard_map/ppermute | solution.py:369
  189.7 17.3 %collective-permute-start.32 = (bf16[128,2048]{1,0:T(8,128)(2,1)}, bf16[128,2048]{1,0:T(8,128)(2,1)S(1)}, u32[]{:S(2)}, u32[]{:S(2)}) collective-permute-start(bf16[128,2048]{1,0:T(8,128)(2,1)} %get-tuple-element.101.refs_0_), channel_id=1, source_target_pairs={{0,32},{32,64},{64,96},{96,0},{1,33},{33,65},{65,97},{97,1},{2,34}... | collective-permute-start | bytes 1572872 | tf_op jit(solution)/shard_map/ppermute | solution.py:81
  189.8 17.4 %collective-permute-start.33 = (bf16[128,2048]{1,0:T(8,128)(2,1)}, bf16[128,2048]{1,0:T(8,128)(2,1)S(1)}, u32[]{:S(2)}, u32[]{:S(2)}) collective-permute-start(bf16[128,2048]{1,0:T(8,128)(2,1)} %get-tuple-element.101.refs_0_), channel_id=1, source_target_pairs={{0,96},{32,0},{64,32},{96,64},{1,97},{33,1},{65,33},{97,65},{2,98}... | collective-permute-start | bytes 1572872 | tf_op jit(solution)/shard_map/ppermute | solution.py:82
  193.1 13.4 %collective-permute-start.43 = (bf16[64,2048]{1,0:T(8,128)(2,1)S(1)}, bf16[64,2048]{1,0:T(8,128)(2,1)S(1)}, u32[]{:S(2)}, u32[]{:S(2)}) collective-permute-start(bf16[64,2048]{1,0:T(8,128)(2,1)S(1)} %slice.169), channel_id=1, source_target_pairs={{0,32},{32,64},{64,96},{96,0},{1,33},{33,65},{65,97},{97,1},{2,34}... | collective-permute-start | bytes 786440 | tf_op jit(solution)/shard_map/ppermute | solution.py:83
  193.1 13.4 %collective-permute-start.44 = (bf16[64,2048]{1,0:T(8,128)(2,1)S(1)}, bf16[64,2048]{1,0:T(8,128)(2,1)S(1)}, u32[]{:S(2)}, u32[]{:S(2)}) collective-permute-start(bf16[64,2048]{1,0:T(8,128)(2,1)S(1)} %slice.170), channel_id=1, source_target_pairs={{0,96},{32,0},{64,32},{96,64},{1,97},{33,1},{65,33},{97,65},{2,98}... | collective-permute-start | bytes 786440 | tf_op jit(solution)/shard_map/ppermute | solution.py:84
  196.4 11.2 %collective-permute-start.45 = (bf16[128,2048]{1,0:T(8,128)(2,1)S(1)}, bf16[128,2048]{1,0:T(8,128)(2,1)S(1)}, u32[]{:S(2)}, u32[]{:S(2)}) collective-permute-start(bf16[128,2048]{1,0:T(8,128)(2,1)S(1)} %bitcast.166), channel_id=1, source_target_pairs={{0,1},{1,0},{2,3},{3,2},{4,5},{5,4},{6,7},{7,6},{8,9},{9,8},{10,11... | collective-permute-start | bytes 1572872 | tf_op jit(solution)/shard_map/ppermute | solution.py:110
  207.6 12.0 %collective-permute-start.36 = (bf16[128,2048]{1,0:T(8,128)(2,1)S(1)}, bf16[128,2048]{1,0:T(8,128)(2,1)S(1)}, u32[]{:S(2)}, u32[]{:S(2)}) collective-permute-start(bf16[128,2048]{1,0:T(8,128)(2,1)S(1)} %copy-done.88), channel_id=1, source_target_pairs={{0,1},{1,0},{2,3},{3,2},{4,5},{5,4},{6,7},{7,6},{8,9},{9,8},{10,11... | collective-permute-start | bytes 1572872 | tf_op jit(solution)/shard_map/ppermute | solution.py:110
  209.5 9.6 %collective-permute-start.34 = (bf16[64,2048]{1,0:T(8,128)(2,1)S(1)}, bf16[64,2048]{1,0:T(8,128)(2,1)S(1)}, u32[]{:S(2)}, u32[]{:S(2)}) collective-permute-start(bf16[64,2048]{1,0:T(8,128)(2,1)S(1)} %slice.167), channel_id=1, source_target_pairs={{0,32},{32,64},{64,96},{96,0},{1,33},{33,65},{65,97},{97,1},{2,34}... | collective-permute-start | bytes 786440 | tf_op jit(solution)/shard_map/ppermute | solution.py:83
  209.9 9.2 %collective-permute-start.35 = (bf16[64,2048]{1,0:T(8,128)(2,1)S(1)}, bf16[64,2048]{1,0:T(8,128)(2,1)S(1)}, u32[]{:S(2)}, u32[]{:S(2)}) collective-permute-start(bf16[64,2048]{1,0:T(8,128)(2,1)S(1)} %slice.168), channel_id=1, source_target_pairs={{0,96},{32,0},{64,32},{96,64},{1,97},{33,1},{65,33},{97,65},{2,98}... | collective-permute-start | bytes 786440 | tf_op jit(solution)/shard_map/ppermute | solution.py:84
  212.9 9.6 %collective-permute-start.38 = (bf16[128,2048]{1,0:T(8,128)(2,1)S(1)}, bf16[128,2048]{1,0:T(8,128)(2,1)}, u32[]{:S(2)}, u32[]{:S(2)}) collective-permute-start(bf16[128,2048]{1,0:T(8,128)(2,1)S(1)} %collective-permute-done.33.refs_2_), channel_id=1, source_target_pairs={{0,1},{1,0},{2,3},{3,2},{4,5},{5,4},{6,7},{7,6},{8,9},{9,8},{10,11... | collective-permute-start | bytes 1572872 | tf_op jit(solution)/shard_map/ppermute | solution.py:110
  275.1 14.2 %collective-permute-start.52 = (bf16[128,2048]{1,0:T(8,128)(2,1)S(1)}, bf16[128,2048]{1,0:T(8,128)(2,1)S(1)}, u32[]{:S(2)}, u32[]{:S(2)}) collective-permute-start(bf16[128,2048]{1,0:T(8,128)(2,1)S(1)} %get-tuple-element.263), channel_id=1, source_target_pairs={{0,96},{32,0},{64,32},{96,64},{1,97},{33,1},{65,33},{97,65},{2,98}... | collective-permute-start | bytes 1572872 | tf_op jit(solution)/shard_map/ppermute | solution.py:365
  277.8 14.9 %collective-permute-start.53 = (bf16[128,2048]{1,0:T(8,128)(2,1)S(1)}, bf16[128,2048]{1,0:T(8,128)(2,1)S(1)}, u32[]{:S(2)}, u32[]{:S(2)}) collective-permute-start(bf16[128,2048]{1,0:T(8,128)(2,1)S(1)} %get-tuple-element.262), channel_id=1, source_target_pairs={{0,32},{32,64},{64,96},{96,0},{1,33},{33,65},{65,97},{97,1},{2,34}... | collective-permute-start | bytes 1572872 | tf_op jit(solution)/shard_map/ppermute | solution.py:366
  306.6 13.6 %collective-permute-start.56 = (bf16[128,2048]{1,0:T(8,128)(2,1)}, bf16[128,2048]{1,0:T(8,128)(2,1)S(1)}, u32[]{:S(2)}, u32[]{:S(2)}) collective-permute-start(bf16[128,2048]{1,0:T(8,128)(2,1)} %get-tuple-element.111.refs_0_), channel_id=1, source_target_pairs={{0,32},{32,64},{64,96},{96,0},{1,33},{33,65},{65,97},{97,1},{2,34}... | collective-permute-start | bytes 1572872 | tf_op jit(solution)/shard_map/ppermute | solution.py:81
  306.8 13.8 %collective-permute-start.57 = (bf16[128,2048]{1,0:T(8,128)(2,1)}, bf16[128,2048]{1,0:T(8,128)(2,1)S(1)}, u32[]{:S(2)}, u32[]{:S(2)}) collective-permute-start(bf16[128,2048]{1,0:T(8,128)(2,1)} %get-tuple-element.111.refs_0_), channel_id=1, source_target_pairs={{0,96},{32,0},{64,32},{96,64},{1,97},{33,1},{65,33},{97,65},{2,98}... | collective-permute-start | bytes 1572872 | tf_op jit(solution)/shard_map/ppermute | solution.py:82
  360.4 9.2 %collective-permute-start.66 = (bf16[512,128]{1,0:T(8,128)(2,1)S(1)}, bf16[512,128]{1,0:T(8,128)(2,1)S(1)}, u32[]{:S(2)}, u32[]{:S(2)}) collective-permute-start(bf16[512,128]{1,0:T(8,128)(2,1)S(1)} %slice.229), channel_id=1, source_target_pairs={{0,16},{16,0},{1,17},{17,1},{2,18},{18,2},{3,19},{19,3},{4,20},{20... | collective-permute-start | bytes 393224 | tf_op jit(solution)/shard_map/ppermute | solution.py:781
  369.1 47.0 %collective-permute-start.60 = (bf16[256,2048]{1,0:T(8,128)(2,1)}, bf16[256,2048]{1,0:T(8,128)(2,1)}, u32[]{:S(2)}, u32[]{:S(2)}) collective-permute-start(bf16[256,2048]{1,0:T(8,128)(2,1)} %get-tuple-element.116), channel_id=1, source_target_pairs={{0,1},{1,0},{2,3},{3,2},{4,5},{5,4},{6,7},{7,6},{8,9},{9,8},{10,11... | collective-permute-start | bytes 3145736 | tf_op jit(solution)/shard_map/ppermute | solution.py:378
  369.2 39.5 %collective-permute-start.61 = (bf16[256,2048]{1,0:T(8,128)(2,1)}, bf16[256,2048]{1,0:T(8,128)(2,1)S(1)}, u32[]{:S(2)}, u32[]{:S(2)}) collective-permute-start(bf16[256,2048]{1,0:T(8,128)(2,1)} %get-tuple-element.118), channel_id=1, source_target_pairs={{0,1},{1,0},{2,3},{3,2},{4,5},{5,4},{6,7},{7,6},{8,9},{9,8},{10,11... | collective-permute-start | bytes 3145736 | tf_op jit(solution)/shard_map/ppermute | solution.py:377
  375.7 15.4 %collective-permute-start.67 = (bf16[128,2048]{1,0:T(8,128)(2,1)}, bf16[128,2048]{1,0:T(8,128)(2,1)S(1)}, u32[]{:S(2)}, u32[]{:S(2)}) collective-permute-start(bf16[128,2048]{1,0:T(8,128)(2,1)} %get-tuple-element.136), channel_id=1, source_target_pairs={{0,96},{32,0},{64,32},{96,64},{1,97},{33,1},{65,33},{97,65},{2,98}... | collective-permute-start | bytes 1572872 | tf_op jit(solution)/shard_map/ppermute | solution.py:365
  380.7 14.9 %collective-permute-start.68 = (bf16[128,2048]{1,0:T(8,128)(2,1)S(1)}, bf16[128,2048]{1,0:T(8,128)(2,1)S(1)}, u32[]{:S(2)}, u32[]{:S(2)}) collective-permute-start(bf16[128,2048]{1,0:T(8,128)(2,1)S(1)} %copy-done.94), channel_id=1, source_target_pairs={{0,32},{32,64},{64,96},{96,0},{1,33},{33,65},{65,97},{97,1},{2,34}... | collective-permute-start | bytes 1572872 | tf_op jit(solution)/shard_map/ppermute | solution.py:366
  381.9 30.5 %collective-permute-start.81 = (bf16[4,4,16,2048]{3,2,1,0:T(8,128)(2,1)}, bf16[4,4,16,2048]{3,2,1,0:T(8,128)(2,1)}, u32[]{:S(2)}, u32[]{:S(2)}) collective-permute-start(bf16[4,4,16,2048]{3,2,1,0:T(8,128)(2,1)} %dynamic-slice_bitcast_fusion.1), channel_id=1, source_target_pairs={{0,1},{1,0},{2,3},{3,2},{4,5},{5,4},{6,7},{7,6},{8,9},{9,8},{10,11... | collective-permute-start | bytes 3145736 | tf_op jit(solution)/shard_map/ppermute | solution.py:761
  391.1 13.0 %collective-permute-start.69 = (bf16[64,2048]{1,0:T(8,128)(2,1)S(1)}, bf16[64,2048]{1,0:T(8,128)(2,1)S(1)}, u32[]{:S(2)}, u32[]{:S(2)}) collective-permute-start(bf16[64,2048]{1,0:T(8,128)(2,1)S(1)} %add_convert_fusion.7), channel_id=1, source_target_pairs={{0,96},{32,0},{64,32},{96,64},{1,97},{33,1},{65,33},{97,65},{2,98}... | collective-permute-start | bytes 786440 | tf_op jit(solution)/shard_map/ppermute | solution.py:369
  395.7 8.6 %collective-permute-start.70 = (bf16[64,2048]{1,0:T(8,128)(2,1)S(1)}, bf16[64,2048]{1,0:T(8,128)(2,1)S(1)}, u32[]{:S(2)}, u32[]{:S(2)}) collective-permute-start(bf16[64,2048]{1,0:T(8,128)(2,1)S(1)} %add_convert_fusion.6), channel_id=1, source_target_pairs={{0,32},{32,64},{64,96},{96,0},{1,33},{33,65},{65,97},{97,1},{2,34}... | collective-permute-start | bytes 786440 | tf_op jit(solution)/shard_map/ppermute | solution.py:369
  404.1 14.0 %collective-permute-start.71 = (bf16[4,4,4,16,768]{4,3,2,1,0:T(8,128)(2,1)S(1)}, bf16[4,4,4,16,768]{4,3,2,1,0:T(8,128)(2,1)S(1)}, u32[]{:S(2)}, u32[]{:S(2)}) collective-permute-start(bf16[4,4,4,16,768]{4,3,2,1,0:T(8,128)(2,1)S(1)} %dynamic-slice_bitcast_fusion), channel_id=1, source_target_pairs={{0,1},{1,0},{2,3},{3,2},{4,5},{5,4},{6,7},{7,6},{8,9},{9,8},{10,11... | collective-permute-start | bytes 4718600 | tf_op jit(solution)/shard_map/ppermute | solution.py:816
  409.1 40.3 %collective-permute-start.62 = (bf16[128,2048]{1,0:T(8,128)(2,1)S(1)}, bf16[128,2048]{1,0:T(8,128)(2,1)S(1)}, u32[]{:S(2)}, u32[]{:S(2)}) collective-permute-start(bf16[128,2048]{1,0:T(8,128)(2,1)S(1)} %get-tuple-element.259), channel_id=1, source_target_pairs={{0,96},{32,0},{64,32},{96,64},{1,97},{33,1},{65,33},{97,65},{2,98}... | collective-permute-start | bytes 1572872 | tf_op jit(solution)/shard_map/ppermute | solution.py:365
  412.3 38.8 %collective-permute-start.63 = (bf16[128,2048]{1,0:T(8,128)(2,1)S(1)}, bf16[128,2048]{1,0:T(8,128)(2,1)S(1)}, u32[]{:S(2)}, u32[]{:S(2)}) collective-permute-start(bf16[128,2048]{1,0:T(8,128)(2,1)S(1)} %get-tuple-element.258), channel_id=1, source_target_pairs={{0,32},{32,64},{64,96},{96,0},{1,33},{33,65},{65,97},{97,1},{2,34}... | collective-permute-start | bytes 1572872 | tf_op jit(solution)/shard_map/ppermute | solution.py:366
  414.1 10.8 %collective-permute-start.84 = (bf16[4,16,2048]{2,1,0:T(8,128)(2,1)S(1)}, bf16[4,16,2048]{2,1,0:T(8,128)(2,1)S(1)}, u32[]{:S(2)}, u32[]{:S(2)}) collective-permute-start(bf16[4,16,2048]{2,1,0:T(8,128)(2,1)S(1)} %get-tuple-element.254), channel_id=1, source_target_pairs={{0,8},{16,24},{8,0},{24,16},{1,9},{17,25},{9,1},{25,17},{2,10},{18... | collective-permute-start | bytes 786440 | tf_op jit(solution)/shard_map/ppermute | solution.py:104
  416.1 14.3 %collective-permute-start.83 = (bf16[4,16,2048]{2,1,0:T(8,128)(2,1)S(1)}, bf16[4,16,2048]{2,1,0:T(8,128)(2,1)S(1)}, u32[]{:S(2)}, u32[]{:S(2)}) collective-permute-start(bf16[4,16,2048]{2,1,0:T(8,128)(2,1)S(1)} %get-tuple-element.255), channel_id=1, source_target_pairs={{0,16},{16,8},{8,24},{24,0},{1,17},{17,9},{9,25},{25,1},{2,18},{18... | collective-permute-start | bytes 786440 | tf_op jit(solution)/shard_map/ppermute | solution.py:103
  418.1 12.8 %collective-permute-start.82 = (bf16[4,16,2048]{2,1,0:T(8,128)(2,1)S(1)}, bf16[4,16,2048]{2,1,0:T(8,128)(2,1)S(1)}, u32[]{:S(2)}, u32[]{:S(2)}) collective-permute-start(bf16[4,16,2048]{2,1,0:T(8,128)(2,1)S(1)} %get-tuple-element.253), channel_id=1, source_target_pairs={{0,24},{16,0},{8,16},{24,8},{1,25},{17,1},{9,17},{25,9},{2,26},{18... | collective-permute-start | bytes 786440 | tf_op jit(solution)/shard_map/ppermute | solution.py:102
  424.9 14.1 %collective-permute-start.74 = (bf16[4,4,16,768]{3,2,1,0:T(8,128)(2,1)S(1)}, bf16[4,4,16,768]{3,2,1,0:T(8,128)(2,1)S(1)}, u32[]{:S(2)}, u32[]{:S(2)}) collective-permute-start(bf16[4,4,16,768]{3,2,1,0:T(8,128)(2,1)S(1)} %get-tuple-element.245), channel_id=1, source_target_pairs={{0,8},{16,24},{8,0},{24,16},{1,9},{17,25},{9,1},{25,17},{2,10},{18... | collective-permute-start | bytes 1179656 | tf_op jit(solution)/shard_map/ppermute | solution.py:104
  430.4 16.2 %collective-permute-start.73 = (bf16[4,4,16,768]{3,2,1,0:T(8,128)(2,1)S(1)}, bf16[4,4,16,768]{3,2,1,0:T(8,128)(2,1)S(1)}, u32[]{:S(2)}, u32[]{:S(2)}) collective-permute-start(bf16[4,4,16,768]{3,2,1,0:T(8,128)(2,1)S(1)} %get-tuple-element.246), channel_id=1, source_target_pairs={{0,16},{16,8},{8,24},{24,0},{1,17},{17,9},{9,25},{25,1},{2,18},{18... | collective-permute-start | bytes 1179656 | tf_op jit(solution)/shard_map/ppermute | solution.py:103
  430.9 15.7 %collective-permute-start.72 = (bf16[4,4,16,768]{3,2,1,0:T(8,128)(2,1)S(1)}, bf16[4,4,16,768]{3,2,1,0:T(8,128)(2,1)S(1)}, u32[]{:S(2)}, u32[]{:S(2)}) collective-permute-start(bf16[4,4,16,768]{3,2,1,0:T(8,128)(2,1)S(1)} %get-tuple-element.244), channel_id=1, source_target_pairs={{0,24},{16,0},{8,16},{24,8},{1,25},{17,1},{9,17},{25,9},{2,26},{18... | collective-permute-start | bytes 1179656 | tf_op jit(solution)/shard_map/ppermute | solution.py:102
  439.0 21.2 %collective-permute-start.87 = (bf16[16,2048]{1,0:T(8,128)(2,1)S(1)}, bf16[16,2048]{1,0:T(8,128)(2,1)S(1)}, u32[]{:S(2)}, u32[]{:S(2)}) collective-permute-start(bf16[16,2048]{1,0:T(8,128)(2,1)S(1)} %get-tuple-element.271), channel_id=1, source_target_pairs={{0,4},{2,6},{4,0},{6,2},{1,5},{3,7},{5,1},{7,3},{8,12},{10,14},{12... | collective-permute-start | bytes 196616 | tf_op jit(solution)/shard_map/ppermute | solution.py:104
  446.6 13.6 %collective-permute-start.86 = (bf16[16,2048]{1,0:T(8,128)(2,1)S(1)}, bf16[16,2048]{1,0:T(8,128)(2,1)S(1)}, u32[]{:S(2)}, u32[]{:S(2)}) collective-permute-start(bf16[16,2048]{1,0:T(8,128)(2,1)S(1)} %get-tuple-element.272), channel_id=1, source_target_pairs={{0,2},{2,4},{4,6},{6,0},{1,3},{3,5},{5,7},{7,1},{8,10},{10,12},{12... | collective-permute-start | bytes 196616 | tf_op jit(solution)/shard_map/ppermute | solution.py:103
  451.1 9.0 %collective-permute-start.75 = (bf16[4,16,768]{2,1,0:T(8,128)(2,1)S(1)}, bf16[4,16,768]{2,1,0:T(8,128)(2,1)S(1)}, u32[]{:S(2)}, u32[]{:S(2)}) collective-permute-start(bf16[4,16,768]{2,1,0:T(8,128)(2,1)S(1)} %get-tuple-element.267), channel_id=1, source_target_pairs={{0,6},{2,0},{4,2},{6,4},{1,7},{3,1},{5,3},{7,5},{8,14},{10,8},{12,... | collective-permute-start | bytes 294920 | tf_op jit(solution)/shard_map/ppermute | solution.py:102
  454.2 9.4 %collective-permute-start.85 = (bf16[16,2048]{1,0:T(8,128)(2,1)S(1)}, bf16[16,2048]{1,0:T(8,128)(2,1)S(1)}, u32[]{:S(2)}, u32[]{:S(2)}) collective-permute-start(bf16[16,2048]{1,0:T(8,128)(2,1)S(1)} %get-tuple-element.270), channel_id=1, source_target_pairs={{0,6},{2,0},{4,2},{6,4},{1,7},{3,1},{5,3},{7,5},{8,14},{10,8},{12,... | collective-permute-start | bytes 196616 | tf_op jit(solution)/shard_map/ppermute | solution.py:102
  457.2 9.0 %collective-permute-start.64 = (bf16[64,2048]{1,0:T(8,128)(2,1)S(1)}, bf16[64,2048]{1,0:T(8,128)(2,1)S(1)}, u32[]{:S(2)}, u32[]{:S(2)}) collective-permute-start(bf16[64,2048]{1,0:T(8,128)(2,1)S(1)} %get-tuple-element.257), channel_id=1, source_target_pairs={{0,96},{32,0},{64,32},{96,64},{1,97},{33,1},{65,33},{97,65},{2,98}... | collective-permute-start | bytes 786440 | tf_op jit(solution)/shard_map/ppermute | solution.py:369
  460.2 11.7 %collective-permute-start.78 = (bf16[16,768]{1,0:T(8,128)(2,1)S(1)}, bf16[16,768]{1,0:T(8,128)(2,1)S(1)}, u32[]{:S(2)}, u32[]{:S(2)}) collective-permute-start(bf16[16,768]{1,0:T(8,128)(2,1)S(1)} %get-tuple-element.277), channel_id=1, source_target_pairs={{0,32},{32,64},{64,96},{96,0},{1,33},{33,65},{65,97},{97,1},{2,34}... | collective-permute-start | bytes 73736 | tf_op jit(solution)/shard_map/ppermute | solution.py:825
  460.3 11.7 %collective-permute-start.79 = (bf16[16,768]{1,0:T(8,128)(2,1)S(1)}, bf16[16,768]{1,0:T(8,128)(2,1)S(1)}, u32[]{:S(2)}, u32[]{:S(2)}) collective-permute-start(bf16[16,768]{1,0:T(8,128)(2,1)S(1)} %get-tuple-element.276), channel_id=1, source_target_pairs={{0,96},{32,0},{64,32},{96,64},{1,97},{33,1},{65,33},{97,65},{2,98}... | collective-permute-start | bytes 73736 | tf_op jit(solution)/shard_map/ppermute | solution.py:826
  (134 other events, 1378.4 us)
Sparse Core Ops, SparseCore 0:
  11.0 101.6 all-gather.1
  271.9 85.7 reduce-scatter.1
